TPU v7x, 256 devices: a whole 4x4x8 slice. The times are simulated.
256 devices in a mesh: dp: 32 (over x, y, core), tensor: 8 (over z).
Axes of the slice: x: 4, y: 4, z: 8, core: 2. Of those that a mesh axis runs over, the one named last changes fastest.
Arguments:
- tokens: bfloat16 [32, 1024, 8192], P('dp', 'tensor'), may hold values from -6 to 6
- cotangent: bfloat16 [32, 1024, 2048], P('dp', None, 'tensor'), may hold values from -0.1875 to 0.1875
- error_buffer: bfloat16 [32, 8192, 2048], P('dp', None, 'tensor'), may hold values from -4 to 4
- start_basis: float32 [2048, 32], P('tensor'), may hold values from -0.125 to 0.125
Outputs:
- decompressed: bfloat16 [8192, 2048], P('dp', 'tensor')
- new_error: bfloat16 [32, 8192, 2048], P('dp', None, 'tensor')
All inputs are finite; a program needn't handle non-finite values.
Results may differ from a plain program's by a relative error of at most 0.00105.
Values may be sent and summed in bfloat16 or wider, within the bound.
No kernel may reach another device: no remote copies, remote signals or barrier semaphores. Data moves between devices by JAX's collectives and lax.ppermute only.
A program may use at most 128 MiB of HBM per device.

v0:
```python
import jax
import jax.numpy as jnp
from jax import lax
from jax.sharding import PartitionSpec as P


def orthonormal(left_factor, gram_matrix):
    triangle = jnp.linalg.cholesky(gram_matrix)
    return lax.linalg.triangular_solve(
        triangle, left_factor, left_side=False, lower=True, transpose_a=True
    )


def shards(tokens, cotangent, error_buffer, start_basis):
    highest = lax.Precision.HIGHEST
    local_tokens = tokens[0]
    own_cotangent = cotangent[0]
    gradient = lax.dot_general(
        lax.all_gather(local_tokens, "tensor", axis=0, tiled=True),
        own_cotangent,
        (((0,), (0,)), ((), ())),
        preferred_element_type=jnp.float32,
    )
    merged = gradient + error_buffer[0].astype(jnp.float32)
    left_part = jnp.dot(merged, start_basis, precision=highest)
    left_factor = lax.psum(left_part, ("dp", "tensor"))
    gram_matrix = lax.dot_general(
        left_factor,
        left_factor,
        (((0,), (0,)), ((), ())),
        precision=highest,
        preferred_element_type=jnp.float32,
    )
    basis = orthonormal(left_factor, gram_matrix)
    right_part = lax.dot_general(
        merged,
        basis,
        (((0,), (0,)), ((), ())),
        precision=highest,
        preferred_element_type=jnp.float32,
    )
    right_factor = lax.psum(right_part, "dp")
    product = lax.dot_general(
        basis,
        right_factor,
        (((1,), (1,)), ((), ())),
        precision=highest,
        preferred_element_type=jnp.float32,
    )
    replicas = lax.axis_size("dp")
    height = product.shape[0] // replicas
    own_rows = lax.dynamic_slice_in_dim(product, lax.axis_index("dp") * height, height, 0)
    decompressed = own_rows.astype(jnp.bfloat16)
    new_error = (merged - product / replicas).astype(jnp.bfloat16)
    return (decompressed, new_error[None])


def solution(mesh):
    in_specs = (
        P("dp", "tensor", None),
        P("dp", None, "tensor"),
        P("dp", None, "tensor"),
        P("tensor", None),
    )
    out_specs = (P("dp", "tensor"), P("dp", None, "tensor"))
    return jax.shard_map(shards, mesh=mesh, in_specs=in_specs, out_specs=out_specs, check_vma=False)
```

profile of v0, /device:TPU:1, one launch (start us, length us, event | category | flops | bytes accessed | tf_op | source)
XLA Modules:
  0.0 640.6 jit_solution(7078342535753091178)
XLA Ops:
  7.2 0.0 copy-start
  7.2 0.0 all-gather.3.cloned.1.call-start
  7.2 0.7 all-gather.3.cloned.1.call-update
  7.9 0.0 copy-start.2
  7.9 0.0 all-reduce.2.cloned.1.call-start
  8.0 178.4 %all-gather.3.cloned.1.call-done = bf16[1,1024,8192]{2,1,0:T(8,128)(2,1)} async-done(((bf16[1,128,8192]{2,1,0:T(8,128)(2,1)}), bf16[1,1024,8192]{2,1,0:T(8,128)(2,1)}) %all-gather.3.cloned.1.call-update) | async-done | bytes 16777232 | tf_op jit(solution)/shard_map/all_gather | solution.py:19
  186.4 0.0 copy-done
  186.4 12.2 %fusion.2 = f32[8192,256]{1,0:T(8,128)S(1)} fusion(bf16[1,1024,8192]{2,1,0:T(8,128)(2,1)} %all-gather.3.cloned.1.call-done, bf16[1,8192,256]{2,1,0:T(8,128)(2,1)} %param.6, bf16[1,1024,256]{2,1,0:T(8,128)(2,1)S(1)} %copy-done), kind=kOutput, calls=%fused_computation.2 | convolution fusion | flops 4299161600 | bytes 29884416 | tf_op jit(solution)/shard_map/dot_general | solution.py:18
  198.6 0.0 copy-start.1
  198.6 3.2 copy-done.1
  201.8 0.0 copy-done.2
  201.8 8.7 %fusion.11 = f32[8192,32]{0,1:T(8,128)} fusion(f32[8192,256]{1,0:T(8,128)S(1)} %fusion.2, f32[256,32]{0,1:T(8,128)S(1)} %copy-done.2), kind=kOutput, calls=%fused_computation.17 | convolution fusion | flops 805306368 | bytes 9469952 | tf_op jit(solution)/shard_map/dot_general | solution.py:25
  210.6 0.0 all-reduce.2.cloned.1.call-update
  210.6 253.2 %all-reduce.2.cloned.1.call-done = f32[8192,32]{0,1:T(8,128)} async-done(((f32[8192,32]{0,1:T(8,128)}), f32[8192,32]{0,1:T(8,128)}) %all-reduce.2.cloned.1.call-update) | async-done | bytes 1048592 | tf_op jit(solution)/shard_map/psum | solution.py:26
  463.8 2.7 fusion.12
  466.5 0.1 copy.6
  466.5 3.0 cholesky.16
  469.6 0.6 compare_reduce_fusion
  470.2 0.7 fusion.7
  470.9 2.4 custom-call.6
  473.3 2.3 fusion.8
  475.6 15.5 %fusion.13 = f32[256,32]{1,0:T(8,128)S(1)} fusion(f32[8192,256]{1,0:T(8,128)} %copy-done.1, f32[8192,32]{0,1:T(8,128)S(1)} %fusion.8), kind=kOutput, calls=%fused_computation.19 | convolution fusion | flops 805306368 | bytes 9469952 | tf_op jit(solution)/shard_map/dot_general | solution.py:35
  491.1 123.1 %psum.15 = f32[256,32]{1,0:T(8,128)S(1)} all-reduce(f32[256,32]{1,0:T(8,128)S(1)} %fusion.13), channel_id=1, replica_groups=mesh['dp'=32,'tensor'=8] {'dp'}, use_global_device_ids=true, to_apply=%region_3.4 | all-reduce | flops 8192 | bytes 65536 | tf_op jit(solution)/shard_map/psum | solution.py:42
  614.2 8.9 %fusion.14 = f32[8192,256]{1,0:T(8,128)} fusion(f32[8192,32]{0,1:T(8,128)S(1)} %fusion.8, f32[256,32]{1,0:T(8,128)S(1)} %psum.15), kind=kOutput, calls=%fused_computation.20 | convolution fusion | flops 805306368 | bytes 9469952 | tf_op jit(solution)/shard_map/dot_general | solution.py:43
  623.1 9.0 %fusion.5 = bf16[1,8192,256]{2,1,0:T(8,128)(2,1)} fusion(f32[8192,256]{1,0:T(8,128)} %copy-done.1, f32[8192,256]{1,0:T(8,128)} %fusion.14), kind=kLoop, calls=%fused_computation.4 | loop fusion | flops 6291456 | bytes 20971520 | tf_op jit(solution)/shard_map/broadcast_in_dim | solution.py:55
  632.1 1.6 dynamic-slice_convert_fusion
  (2 shorter events, 0.0 us)
Async XLA Ops:
  7.2 179.2 %copy-start = (bf16[1,1024,256]{2,1,0:T(8,128)(2,1)S(1)}, bf16[1,1024,256]{2,1,0:T(8,128)(2,1)}, u32[]{:S(2)}) copy-start(bf16[1,1024,256]{2,1,0:T(8,128)(2,1)} %param.5) | copy-start | bytes 1572868
  7.2 179.2 %all-gather.3.cloned.1.call-start = ((), (), s32[]{:S(2)}) async-start(), calls=%async_computation.1 | async-start | bytes 18874368 | tf_op jit(solution)/shard_map/all_gather | solution.py:19
  7.9 193.9 %copy-start.2 = (f32[256,32]{0,1:T(8,128)S(1)}, f32[256,32]{0,1:T(8,128)}, u32[]{:S(2)}) copy-start(f32[256,32]{0,1:T(8,128)} %param.7) | copy-start | bytes 98308
  7.9 455.8 %all-reduce.2.cloned.1.call-start = ((), (), s32[]{:S(2)}) async-start(), calls=%async_computation | async-start | bytes 2097152 | tf_op jit(solution)/shard_map/psum | solution.py:26
  198.6 3.2 copy-start.1
Sparse Core Ops, SparseCore 0:
  9.8 176.5 all-gather.2
  210.7 253.0 all-reduce.1
where the time goes:
time: 644 us; the launch traced here: 641 us
  waiting for transfers between devices  432 us (67%)
  blocking collectives  123 us (19%)
  matrix products  50.3 us (8%)
  other arithmetic  15.8 us (2%)
  between operations  14.1 us (2%)
    psum x1, waiting for transfers between devices, shards(): left_factor = lax.psum(left_part, ('dp', 'tensor'))  253 us
    all_gather x1, waiting for transfers between devices, shards(): lax.all_gather(local_tokens, 'tensor', axis=0, tiled=True)  178 us
    psum x1, blocking collectives, shards(): right_factor = lax.psum(right_part, 'dp')  123 us
    dot_general x1, matrix products, shards(): lax.dot_general(merged, basis, (((0,), (0,)), ((), ())), precision=highes...  15.5 us
  transfers between devices with their start and end apart: 2, of which 2 were waited for; matrix products, arithmetic and copies ran while one was open for 0% of the time, Pallas kernels for 0%

commit v1 on v0

v1 whole, which is shorter than its diff:
```python
import jax
import jax.numpy as jnp
from jax import lax
from jax.experimental import pallas as pl
from jax.experimental.pallas import tpu as pltpu
from jax.sharding import PartitionSpec as P

F32 = jnp.float32
BF16 = jnp.bfloat16
GATHERED = 8
CHUNKS = 8
DEEP = 2
TIES = (-1, -1, -1, -1, -1, -1)
TILE = 1024
BUFFERS = 2
VMEM = 56 << 20


def split(x):
    high = lax.reduce_precision(x, 8, 7)
    rest = x - high
    middle = lax.reduce_precision(rest, 8, 7)
    return high.astype(BF16), middle.astype(BF16), (rest - middle).astype(BF16)


def split_rows(x):
    return jnp.concatenate(split(x), axis=0)


def join_rows(x):
    rank = x.shape[0] // 3
    return (x[2 * rank :] + x[rank : 2 * rank]) + x[:rank]


def dot(a, b, dims):
    return lax.dot_general(a, b, (dims, ((), ())), preferred_element_type=F32)


def shift(x, axis, by):
    size = lax.axis_size(axis)
    return lax.ppermute(x, axis, [(j, (j + by) % size) for j in range(size)])


def after(x, *others):
    return lax.optimization_barrier((x,) + others)[0] if others else x


def ring(own, axis, deep):
    size = lax.axis_size(axis)
    half = size // 2
    up, down = list(own), list(own)
    blocks = [[piece] + [None] * (size - 1) for piece in own]
    ups, downs = [], []
    for hop in range(1, half + 1):
        for c in range(len(own)):
            if hop < half or c % 2 == 0:
                up[c] = shift(after(up[c], ups[-deep]) if len(ups) >= deep else up[c], axis, 1)
                blocks[c][size - hop] = up[c]
                ups.append(up[c])
            if hop < half or c % 2 == 1:
                down[c] = shift(after(down[c], downs[-deep]) if len(downs) >= deep else down[c], axis, -1)
                blocks[c][hop] = down[c]
                downs.append(down[c])
    return blocks, list(zip(ups, downs))


def finish_kernel(count, *refs):
    blocks, (cot_ref, right_ref, basis_ref, error_ref), out_ref = refs[:count], refs[count : count + 4], refs[-1]
    if count == 1:
        whole = blocks[0][...]
    else:
        whole = jnp.concatenate([block[...] for block in blocks], axis=0)
    total = dot(basis_ref[...], right_ref[...], ((0,), (0,))) + dot(whole, cot_ref[...], ((0,), (0,)))
    out_ref[...] = (total + error_ref[...].astype(F32)).astype(BF16)


def finish(start, blocks, cot, right_wide, basis_wide, error, out):
    count = len(blocks)
    depth, width = blocks[0].shape
    rows, columns = error.shape
    tile = TILE
    inside = cot.shape[0]
    extra = right_wide.shape[0]
    at = lambda i: start // tile + i
    deep = dict(pipeline_mode=pl.Buffered(BUFFERS)) if width // tile > 2 else {}
    in_specs = [pl.BlockSpec((depth, tile), lambda i: (0, i), **deep) for _ in range(count)] + [
        pl.BlockSpec((inside, columns), lambda i: (0, 0)),
        pl.BlockSpec((extra, columns), lambda i: (0, 0)),
        pl.BlockSpec((extra, tile), lambda i: (0, at(i)), **deep),
        pl.BlockSpec((tile, columns), lambda i: (at(i), 0), **deep),
    ]
    operands = list(blocks) + [cot, right_wide, basis_wide, error]
    aliases = {}
    if out is not None:
        in_specs.append(pl.BlockSpec(memory_space=pl.ANY))
        operands.append(out)
        aliases = {len(operands) - 1: 0}
    return pl.pallas_call(
        lambda *refs: finish_kernel(count, *refs),
        grid=(width // tile,),
        in_specs=in_specs,
        out_specs=pl.BlockSpec((tile, columns), lambda i: (at(i), 0)),
        out_shape=jax.ShapeDtypeStruct((rows, columns), BF16),
        input_output_aliases=aliases,
        compiler_params=pltpu.CompilerParams(vmem_limit_bytes=VMEM),
        cost_estimate=pl.CostEstimate(
            flops=2 * inside * width * columns, bytes_accessed=2 * width * (inside + 2 * columns), transcendentals=0
        ),
    )(*operands)


def gather(x, axis):
    return lax.all_to_all(jnp.broadcast_to(x, (lax.axis_size(axis),) + x.shape), axis, 0, 0)


def shards(tokens, cotangent, error_buffer, start_basis):
    highest = lax.Precision.HIGHEST
    tokens, cot, error = tokens[0], cotangent[0], error_buffer[0]
    planes = lax.axis_size("tensor")
    replicas = lax.axis_size("dp")
    depth, d = tokens.shape
    columns, rank = start_basis.shape
    width = d // CHUNKS
    cut = GATHERED * width
    if GATHERED > 0:
        gathered = lax.all_gather(tokens[:, :cut], "tensor", axis=0, tiled=True)
    blocks, events = ring([tokens[:, c * width : (c + 1) * width] for c in range(GATHERED, CHUNKS)], "tensor", DEEP)

    def tie(x, stage):
        return after(x, *events[TIES[stage]]) if TIES[stage] >= 0 else x

    start3 = split_rows(start_basis.T)
    weights = join_rows(dot(start3, cot, ((1,), (1,))))
    weights = weights.reshape(rank, planes, depth).transpose(1, 0, 2)
    weight = tie(jnp.sum(lax.all_to_all(weights, "tensor", 0, 0), axis=0), 0)
    left_part = join_rows(dot(split_rows(weight), tokens, ((1,), (0,))) + dot(start3, error, ((1,), (1,))))
    height = d // replicas
    left_part = left_part.reshape(rank, replicas, height).transpose(1, 0, 2)
    left_rows = jnp.sum(lax.all_to_all(left_part, "dp", 0, 0), axis=0)
    left_rows = tie(left_rows, 1)
    whole_rows = tie(jnp.sum(gather(left_rows, "tensor"), axis=0), 2)
    left = gather(whole_rows, "dp").transpose(1, 0, 2).reshape(rank, d)
    left = tie(left, 3)

    left3 = split_rows(left)
    inner = join_rows(dot(left3, tokens, ((1,), (1,))))
    inner = gather(inner, "tensor").transpose(1, 0, 2).reshape(rank, planes * depth)
    inner = tie(inner, 4)
    right_part = join_rows(dot(split_rows(inner), cot, ((1,), (0,))) + dot(left3, error, ((1,), (0,))))
    right = tie(jnp.sum(gather(right_part, "dp"), axis=0), 5)

    gram = lax.dot_general(left, left, (((1,), (1,)), ((), ())), precision=highest, preferred_element_type=F32)
    triangle = jnp.linalg.cholesky(gram)
    inverse = lax.linalg.triangular_solve(triangle, jnp.eye(rank, dtype=F32), left_side=True, lower=True)
    basis = jnp.dot(inverse, left, precision=highest)
    right = jnp.dot(inverse, right, precision=highest)

    mine = lax.dynamic_slice_in_dim(basis, lax.axis_index("dp") * height, height, 1)
    decompressed = lax.dot_general(
        mine, right, (((0,), (0,)), ((), ())), precision=highest, preferred_element_type=F32
    ).astype(BF16)

    bh, bm, bl = split(basis)
    rh, rm, rl = split(right * (-1.0 / replicas))
    basis_wide = jnp.concatenate([bh, bm, bh, bm, bl, bh], axis=0)
    right_wide = jnp.concatenate([rh, rh, rm, rm, rh, rl], axis=0)
    out = None
    if GATHERED < CHUNKS:
        place = lax.axis_index("tensor") * depth
        turned = lax.dynamic_slice_in_dim(jnp.concatenate([cot, cot], axis=0), place, planes * depth, 0)
        for c, piece in enumerate(blocks):
            out = finish((GATHERED + c) * width, piece, turned, right_wide, basis_wide, error, out)
    if GATHERED > 0:
        out = finish(0, [gathered], cot, right_wide, basis_wide, error, out)
    return decompressed, out[None]


def solution(mesh):
    in_specs = (
        P("dp", "tensor", None),
        P("dp", None, "tensor"),
        P("dp", None, "tensor"),
        P("tensor", None),
    )
    out_specs = (P("dp", "tensor"), P("dp", None, "tensor"))
    return jax.shard_map(shards, mesh=mesh, in_specs=in_specs, out_specs=out_specs, check_vma=False)
```

time: 644 us -> 217 us (0.34)
  waiting for transfers between devices: 432 us -> 83.7 us
  blocking collectives: 123 us -> 59.9 us
  matrix products: 50.3 us -> 13.2 us
  Pallas kernels: 0 us -> 14.3 us
  starting transfers between devices: 0.08 us -> 12.4 us
    psum x1 -> x0, waiting for transfers between devices: 253 us -> none  [shards(): left_factor = lax.psum(left_part, ('dp', 'tensor'))]
    all_gather x1, waiting for transfers between devices: 178 us -> 44.8 us  [shards(): gathered = lax.all_gather(tokens[:, :cut], 'tensor', axis=0, tiled=True)]
    psum x1 -> x0, blocking collectives: 123 us -> none  [shards(): right_factor = lax.psum(right_part, 'dp')]
    all_to_all x0 -> x3, blocking collectives: none -> 59.9 us  [the longest x1 26 us: shards(): left_rows = jnp.sum(lax.all_to_all(left_part, 'dp', 0, 0), axis=0)]
    all_to_all x0 -> x3, waiting for transfers between devices: none -> 38.2 us  [gather(): lax.all_to_all(jnp.broadcast_to(x, (lax.axis_size(axis),) + x.shape), axi...]
    dot_general x5 -> x10, matrix products: 48.1 us -> 13 us  [the longest x6 8.94 us: dot(): return lax.dot_general(a, b, (dims, ((), ())), preferred_element_type=F32)]
    pallas_call x0 -> x1, Pallas kernels: none -> 14.3 us  [finish(): pl.pallas_call(lambda *refs: finish_kernel(count, *refs), grid=(width //...]
    all_to_all x0 -> x3, starting transfers between devices: none -> 12.4 us  [gather(): lax.all_to_all(jnp.broadcast_to(x, (lax.axis_size(axis),) + x.shape), axi...]
  transfers between devices with their start and end apart: 2 -> 4, of which waited for: 2 -> 4; matrix products, arithmetic and copies ran while one was open for 0% -> 13% of each run, Pallas kernels for 0% -> 0%
where the time goes in v1:
time: 217 us; the launch traced here: 216 us
  waiting for transfers between devices  83.7 us (39%)
  blocking collectives  59.9 us (28%)
  Pallas kernels  14.3 us (7%)
  between operations  14.3 us (7%)
  matrix products  13.2 us (6%)
  other arithmetic  12.5 us (6%)
  starting transfers between devices  12.4 us (6%)
  local copies, waits for them, and re-layouts  5.66 us (3%)
    all_gather x1, waiting for transfers between devices, shards(): gathered = lax.all_gather(tokens[:, :cut], 'tensor', axis=0, tiled=True)  44.8 us
    all_to_all x3, waiting for transfers between devices, gather(): lax.all_to_all(jnp.broadcast_to(x, (lax.axis_size(axis),) + x.shape), axi...  38.2 us
    all_to_all x1, blocking collectives, shards(): left_rows = jnp.sum(lax.all_to_all(left_part, 'dp', 0, 0), axis=0)  26 us
    all_to_all x1, blocking collectives, gather(): lax.all_to_all(jnp.broadcast_to(x, (lax.axis_size(axis),) + x.shape), axi...  17.4 us
    all_to_all x1, blocking collectives, shards(): weight = tie(jnp.sum(lax.all_to_all(weights, 'tensor', 0, 0), axis=0), 0)  16.6 us
    pallas_call x1, Pallas kernels, finish(): pl.pallas_call(lambda *refs: finish_kernel(count, *refs), grid=(width //...  14.3 us
    all_to_all x3, starting transfers between devices, gather(): lax.all_to_all(jnp.broadcast_to(x, (lax.axis_size(axis),) + x.shape), axi...  12.4 us
    dot_general x6, matrix products, dot(): return lax.dot_general(a, b, (dims, ((), ())), preferred_element_type=F32)  8.94 us
  transfers between devices with their start and end apart: 4, of which 4 were waited for; matrix products, arithmetic and copies ran while one was open for 13% of the time, Pallas kernels for 0%

profile of v1, /device:TPU:1, one launch (start us, length us, event | category | flops | bytes accessed | tf_op | source)
XLA Modules:
  0.0 216.0 jit_solution(728625740776197312)
XLA Ops:
  7.2 0.0 copy-start.1
  7.2 0.0 all-gather.3.cloned.1.call-start
  7.2 0.7 all-gather.3.cloned.1.call-update
  7.9 0.8 reduce-precision_convert_fusion.9
  8.7 1.3 fusion.26
  10.0 16.6 %all_to_all.30 = f32[8,32,128]{2,1,0:T(8,128)S(1)} all-to-all(f32[8,32,128]{2,1,0:T(8,128)S(1)} %bitcast_bitcast_fusion.1), channel_id=1, replica_groups=mesh['dp'=32,'tensor'=8] {'tensor'}, dimensions={0} | all-to-all | bytes 262144 | tf_op jit(solution)/shard_map/all_to_all | solution.py:135
  26.6 0.0 copy-start
  26.7 0.6 fusion.2
  27.3 1.7 copy-done
  28.9 1.4 convolution_add_fusion
  30.3 0.2 slice_add_fusion
  30.5 0.1 copy.31
  30.6 26.0 %all_to_all.31 = f32[32,32,256]{2,1,0:T(8,128)S(1)} all-to-all(f32[32,32,256]{2,1,0:T(8,128)S(1)} %bitcast.75), channel_id=1, replica_groups=mesh['dp'=32,'tensor'=8] {'dp'}, dimensions={0} | all-to-all | bytes 2097152 | tf_op jit(solution)/shard_map/all_to_all | solution.py:139
  56.6 0.1 reduce_sum.37
  56.7 17.4 %all_to_all.32 = f32[8,32,256]{2,1,0:T(8,128)S(1)} all-to-all(f32[8,32,256]{2,1,0:T(8,128)S(1)} %broadcast_in_dim.17), channel_id=1, replica_groups=mesh['dp'=32,'tensor'=8] {'tensor'}, dimensions={0} | all-to-all | bytes 524288 | tf_op jit(solution)/shard_map/all_to_all | solution.py:113
  74.1 1.1 broadcast_in_dim.18
  75.2 4.5 %all-to-all-start.3 = ((f32[32,32,256]{2,1,0:T(8,128)}), f32[32,32,256]{2,1,0:T(8,128)S(1)}, u32[]{:S(2)}, u32[]{:S(2)}) async-start(f32[32,32,256]{2,1,0:T(8,128)} %broadcast_in_dim.18), calls=%async_computation.3 | async-start | bytes 2097152 | tf_op jit(solution)/shard_map/all_to_all | solution.py:113
  79.7 17.0 %all-to-all-done.3 = f32[32,32,256]{2,1,0:T(8,128)S(1)} async-done(((f32[32,32,256]{2,1,0:T(8,128)}), f32[32,32,256]{2,1,0:T(8,128)S(1)}, u32[]{:S(2)}, u32[]{:S(2)}) %all-to-all-start.3) | async-done | bytes 1048608 | tf_op jit(solution)/shard_map/all_to_all | solution.py:113
  96.7 1.0 convolution_bitcast_fusion
  97.6 0.1 copy.16
  97.7 2.9 %cholesky.17 = f32[32,32]{1,0:T(8,128)S(1)} custom-call(f32[32,32]{1,0:T(8,128)S(1)} %fusion.31), custom_call_target="Cholesky" | custom-call | tf_op jit(solution)/shard_map/jit(cholesky)/cholesky | solution.py:153
  100.6 0.6 compare_reduce_fusion
  101.3 0.7 fusion.27
  102.0 2.4 %custom-call.6 = f32[1,32,32]{1,2,0:T(8,128)S(1)} custom-call(f32[1,32,32]{2,1,0:T(8,128)S(1)} %fusion.27), custom_call_target="InvertDiagBlocksLowerTriangular" | custom-call | tf_op jit(solution)/shard_map/triangular_solve | solution.py:154
  104.4 0.1 copy.21
  104.5 0.2 reduce-precision_convert_fusion.3
  104.7 0.8 copy-done.5
  105.5 2.4 %fusion = f32[96,128]{1,0:T(8,128)S(1)} fusion(bf16[1,128,8192]{2,1,0:T(8,128)(2,1)} %param.4, bf16[32,8192]{1,0:T(8,128)(2,1)S(1)} %get-tuple-element.3, bf16[32,8192]{1,0:T(8,128)(2,1)S(1)} %get-tuple-element.4, bf16[32,8192]{1,0:T(8,128)(2,1)S(1)} %get-tuple-element.2), kind=kOutput, calls=%fused_computation.1 | convolution fusion | flops 206045184 | bytes 3719168 | tf_op jit(solution)/shard_map/dot_general | solution.py:36
  107.9 0.7 broadcast_in_dim.19
  108.6 3.4 %all-to-all-start.4 = ((f32[8,32,128]{2,1,0:T(8,128)}), f32[8,32,128]{2,1,0:T(8,128)S(1)}, u32[]{:S(2)}, u32[]{:S(2)}) async-start(f32[8,32,128]{2,1,0:T(8,128)} %broadcast_in_dim.19), calls=%async_computation.4 | async-start | bytes 262144 | tf_op jit(solution)/shard_map/all_to_all | solution.py:113
  112.0 0.2 fusion.29
  112.2 1.8 constant_dynamic-update-slice_fusion.8
  114.0 0.9 fusion.16
  114.9 0.9 constant_dynamic-update-slice_fusion.7
  115.7 0.9 fusion.17
  116.6 1.0 fusion.7
  117.6 5.1 %all-to-all-done.4 = f32[8,32,128]{2,1,0:T(8,128)S(1)} async-done(((f32[8,32,128]{2,1,0:T(8,128)}), f32[8,32,128]{2,1,0:T(8,128)S(1)}, u32[]{:S(2)}, u32[]{:S(2)}) %all-to-all-start.4) | async-done | bytes 131104 | tf_op jit(solution)/shard_map/all_to_all | solution.py:113
  122.7 0.2 fusion.8
  122.9 3.1 %convolution_add_fusion.1 = f32[96,256]{1,0:T(8,128)S(1)} fusion(f32[96,256]{1,0:T(8,128)S(1)} %fusion.8, bf16[32,8192]{1,0:T(8,128)(2,1)S(1)} %copy-done.4, bf16[32,8192]{1,0:T(8,128)(2,1)S(1)} %copy-done.6, bf16[32,8192]{1,0:T(8,128)(2,1)S(1)} %get-tuple-element.2, bf16[1,8192,256]{2,1,0:T(8,128)(2,1)} %param.6), kind=kOutput, calls=%fused_computation.15 | convolution fusion | flops 407396352 | bytes 5963776 | tf_op jit(solution)/shard_map/dot_general | solution.py:36
  126.0 1.1 broadcast_in_dim.20
  127.1 4.5 %all-to-all-start.5 = ((f32[32,32,256]{2,1,0:T(8,128)}), f32[32,32,256]{2,1,0:T(8,128)S(1)}, u32[]{:S(2)}, u32[]{:S(2)}) async-start(f32[32,32,256]{2,1,0:T(8,128)} %broadcast_in_dim.20), calls=%async_computation.5 | async-start | bytes 2097152 | tf_op jit(solution)/shard_map/all_to_all | solution.py:113
  131.6 0.9 constant_dynamic-update-slice_fusion.6.refs_3_
  132.4 16.1 %all-to-all-done.5 = f32[32,32,256]{2,1,0:T(8,128)S(1)} async-done(((f32[32,32,256]{2,1,0:T(8,128)}), f32[32,32,256]{2,1,0:T(8,128)S(1)}, u32[]{:S(2)}, u32[]{:S(2)}) %all-to-all-start.5) | async-done | bytes 1048608 | tf_op jit(solution)/shard_map/all_to_all | solution.py:113
  148.6 0.1 reduce_sum.39
  148.7 0.2 constant_dynamic-update-slice_fusion.5
  148.9 1.1 convolution_convert_fusion
  150.0 44.8 %all-gather.3.cloned.1.call-done = bf16[1,1024,8192]{2,1,0:T(8,128)(2,1)} async-done(((bf16[1,128,8192]{2,1,0:T(8,128)(2,1)}), bf16[1,1024,8192]{2,1,0:T(8,128)(2,1)}) %all-gather.3.cloned.1.call-update) | async-done | bytes 16777232 | tf_op jit(solution)/shard_map/all_gather | solution.py:126
  194.8 14.3 %shard_map.59 = bf16[8192,256]{1,0:T(8,128)(2,1)} custom-call(bf16[1024,8192]{1,0:T(8,128)(2,1)} %bitcast.70, bf16[1024,256]{1,0:T(8,128)(2,1)} %bitcast.78, bf16[192,256]{1,0:T(8,128)(2,1)} %copy-done.7, bf16[192,8192]{1,0:T(8,128)(2,1)} %constant_dynamic-update-slice_fusion.6.refs_3_, bf16[8192,256]{1,0:T(8,128)(2,1)} %bitcast.71), custom_call_target="tpu_custom_call" | custom-call | flops 4294967296 | bytes 25165824 | tf_op jit(solution)/shard_map/pallas_call | solution.py:98
  (27 shorter events, 0.2 us)
Async XLA Ops:
  7.2 19.5 %copy-start.1 = (bf16[1,128,8192]{2,1,0:T(8,128)(2,1)S(1)}, bf16[1,128,8192]{2,1,0:T(8,128)(2,1)}, u32[]{:S(2)}) copy-start(bf16[1,128,8192]{2,1,0:T(8,128)(2,1)} %param.4) | copy-start | bytes 6291460
  7.2 187.6 %all-gather.3.cloned.1.call-start = ((), (), s32[]{:S(2)}) async-start(), calls=%async_computation.6 | async-start | bytes 18874368 | tf_op jit(solution)/shard_map/all_gather | solution.py:126
  26.6 2.3 %copy-start = (bf16[1,8192,256]{2,1,0:T(8,128)(2,1)S(1)}, bf16[1,8192,256]{2,1,0:T(8,128)(2,1)}, u32[]{:S(2)}) copy-start(bf16[1,8192,256]{2,1,0:T(8,128)(2,1)} %param.6) | copy-start | bytes 12582916
  75.2 21.5 %all-to-all-start.3 = ((f32[32,32,256]{2,1,0:T(8,128)}), f32[32,32,256]{2,1,0:T(8,128)S(1)}, u32[]{:S(2)}, u32[]{:S(2)}) async-start(f32[32,32,256]{2,1,0:T(8,128)} %broadcast_in_dim.18), calls=%async_computation.3 | async-start | bytes 2097152 | tf_op jit(solution)/shard_map/all_to_all | solution.py:113
  104.7 0.8 copy-start.5
  104.7 3.9 %copy-start.3 = (bf16[32,8192]{1,0:T(8,128)(2,1)}, bf16[32,8192]{1,0:T(8,128)(2,1)S(1)}, u32[]{:S(2)}) copy-start(bf16[32,8192]{1,0:T(8,128)(2,1)S(1)} %get-tuple-element.3) | copy-start | bytes 1572868
  108.6 14.0 %all-to-all-start.4 = ((f32[8,32,128]{2,1,0:T(8,128)}), f32[8,32,128]{2,1,0:T(8,128)S(1)}, u32[]{:S(2)}, u32[]{:S(2)}) async-start(f32[8,32,128]{2,1,0:T(8,128)} %broadcast_in_dim.19), calls=%async_computation.4 | async-start | bytes 262144 | tf_op jit(solution)/shard_map/all_to_all | solution.py:113
  114.0 8.7 %copy-start.2 = (bf16[1,1024,256]{2,1,0:T(8,128)(2,1)S(1)}, bf16[1,1024,256]{2,1,0:T(8,128)(2,1)}, u32[]{:S(2)}) copy-start(bf16[1,1024,256]{2,1,0:T(8,128)(2,1)} %param.5) | copy-start | bytes 1572868
  114.9 8.0 %copy-start.4 = (bf16[32,8192]{1,0:T(8,128)(2,1)S(1)}, bf16[32,8192]{1,0:T(8,128)(2,1)}, u32[]{:S(2)}) copy-start(bf16[32,8192]{1,0:T(8,128)(2,1)} %copy-done.3) | copy-start | bytes 1572868
  114.9 8.0 %copy-start.6 = (bf16[32,8192]{1,0:T(8,128)(2,1)S(1)}, bf16[32,8192]{1,0:T(8,128)(2,1)}, u32[]{:S(2)}) copy-start(bf16[32,8192]{1,0:T(8,128)(2,1)} %copy-done.5) | copy-start | bytes 1572868
  127.1 21.5 %all-to-all-start.5 = ((f32[32,32,256]{2,1,0:T(8,128)}), f32[32,32,256]{2,1,0:T(8,128)S(1)}, u32[]{:S(2)}, u32[]{:S(2)}) async-start(f32[32,32,256]{2,1,0:T(8,128)} %broadcast_in_dim.20), calls=%async_computation.5 | async-start | bytes 2097152 | tf_op jit(solution)/shard_map/all_to_all | solution.py:113
  148.9 45.9 %copy-start.7 = (bf16[192,256]{1,0:T(8,128)(2,1)}, bf16[192,256]{1,0:T(8,128)(2,1)S(1)}, u32[]{:S(2)}) copy-start(bf16[192,256]{1,0:T(8,128)(2,1)S(1)} %constant_dynamic-update-slice_fusion.refs_2_) | copy-start | bytes 294916
Sparse Core Ops, SparseCore 0:
  9.8 184.9 all-gather.2

commit v2 on v0

v2 whole, which is shorter than its diff:
```python
import jax
import jax.numpy as jnp
from jax import lax
from jax.experimental import pallas as pl
from jax.experimental.pallas import tpu as pltpu
from jax.sharding import PartitionSpec as P

F32 = jnp.float32
BF16 = jnp.bfloat16
CHUNKS = 2
TILE = 1024
LAST = 2048


def split(x):
    high = lax.reduce_precision(x, 8, 7)
    rest = x - high
    middle = lax.reduce_precision(rest, 8, 7)
    return high.astype(BF16), middle.astype(BF16), (rest - middle).astype(BF16)


def split_rows(x):
    return jnp.concatenate(split(x), axis=0)


def join_rows(x):
    rank = x.shape[0] // 3
    return (x[2 * rank :] + x[rank : 2 * rank]) + x[:rank]


def dot(a, b, dims):
    return lax.dot_general(a, b, (dims, ((), ())), preferred_element_type=F32)


def shift(x, axis, by):
    size = lax.axis_size(axis)
    return lax.ppermute(x, axis, [(j, (j + by) % size) for j in range(size)])


def after(x, *others):
    return lax.optimization_barrier((x,) + others)[0] if others else x


class Ring:

    def __init__(self, own, axis):
        self.axis, self.size = axis, lax.axis_size(axis)
        half = self.size // 2
        self.up, self.down = list(own), list(own)
        self.blocks = [[piece] + [None] * (self.size - 1) for piece in own]
        ways = [(hop, c) for hop in range(1, half + 1) for c in range(len(own))]
        self.ups = [(hop, c) for hop, c in ways if hop < half or c % 2 == 0]
        self.downs = [(hop, c) for hop, c in ways if hop < half or c % 2 == 1]

    def step(self, *gate):
        hop, c = self.ups.pop(0)
        self.up[c] = first = shift(after(self.up[c], *gate), self.axis, 1)
        self.blocks[c][self.size - hop] = first
        hop, c = self.downs.pop(0)
        self.down[c] = second = shift(after(self.down[c], *gate), self.axis, -1)
        self.blocks[c][hop] = second
        return first, second


def solve_kernel(left_ref, parts_ref, answer_ref, wide_ref):
    rank = parts_ref.shape[1]
    gram = jnp.zeros((rank, rank), F32)
    for k in (2, 1, 0):
        block = dot(left_ref[...], left_ref[k * rank : (k + 1) * rank, :], ((1,), (1,)))
        gram += join_rows(block)
    row = lax.broadcasted_iota(jnp.int32, (rank, 2 * rank), 0)
    column = lax.broadcasted_iota(jnp.int32, (rank, 2 * rank), 1)
    eye = jnp.where(row + rank == column, 1.0, 0.0).astype(F32)
    both = jnp.concatenate([gram, eye[:, rank:]], axis=1)
    for j in range(rank):
        spread_column = jnp.broadcast_to(both[:, j : j + 1], both.shape)
        scaled = both[j : j + 1, :] / spread_column[j : j + 1, :]
        both = both - jnp.where(row > j, spread_column, 0.0) * scaled
    pivots = jnp.sum(jnp.where(row == column, both, 0.0), axis=1, keepdims=True)
    inverse = both[:, rank:] * (1.0 / jnp.sqrt(pivots))
    total = jnp.sum(parts_ref[...], axis=0)
    exact = dict(precision=lax.Precision.HIGHEST, preferred_element_type=F32)
    right = lax.dot_general(inverse, total, (((1,), (0,)), ((), ())), **exact)
    answer = lax.dot_general(inverse.T, right, (((1,), (0,)), ((), ())), **exact)
    answer_ref[...] = answer
    share = answer * (-1.0 / parts_ref.shape[0])
    high = share.astype(BF16)
    rest = share - high.astype(F32)
    middle = rest.astype(BF16)
    low = (rest - middle.astype(F32)).astype(BF16)
    wide_ref[...] = jnp.concatenate([high, high, middle, middle, high, low], axis=0)


def solve(left3, parts):
    _, rank, columns = parts.shape
    return pl.pallas_call(
        solve_kernel,
        out_shape=(
            jax.ShapeDtypeStruct((rank, columns), F32),
            jax.ShapeDtypeStruct((6 * rank, columns), BF16),
        ),
        compiler_params=pltpu.CompilerParams(vmem_limit_bytes=24 << 20),
        cost_estimate=pl.CostEstimate(flops=1 << 24, bytes_accessed=3 << 20, transcendentals=0),
    )(left3, parts)


def partial_kernel(count, *refs):
    blocks, (cot_ref, right_ref, left_ref, error_ref), out_ref = refs[:count], refs[count : count + 4], refs[-1]
    rank = left_ref.shape[0] // 3
    high, middle, low = (left_ref[k * rank : (k + 1) * rank, :] for k in range(3))
    left = jnp.concatenate([high, middle, high, middle, low, high], axis=0)
    whole = jnp.concatenate([block[...] for block in blocks], axis=0)
    total = dot(left, right_ref[...], ((0,), (0,))) + dot(whole, cot_ref[...], ((0,), (0,)))
    out_ref[...] = total + error_ref[...].astype(F32)


def partial(start, blocks, cot, right_wide, left3, error):
    count = len(blocks)
    depth, width = blocks[0].shape
    columns = error.shape[1]
    inside, extra = cot.shape[0], right_wide.shape[0]
    at = lambda i: start // TILE + i
    return pl.pallas_call(
        lambda *refs: partial_kernel(count, *refs),
        grid=(width // TILE,),
        in_specs=[pl.BlockSpec((depth, TILE), lambda i: (0, i)) for _ in range(count)]
        + [
            pl.BlockSpec((inside, columns), lambda i: (0, 0)),
            pl.BlockSpec((extra, columns), lambda i: (0, 0)),
            pl.BlockSpec((extra // 2, TILE), lambda i: (0, at(i))),
            pl.BlockSpec((TILE, columns), lambda i: (at(i), 0)),
        ],
        out_specs=pl.BlockSpec((TILE, columns), lambda i: (i, 0)),
        out_shape=jax.ShapeDtypeStruct((width, columns), F32),
        compiler_params=pltpu.CompilerParams(vmem_limit_bytes=24 << 20),
        cost_estimate=pl.CostEstimate(
            flops=2 * inside * width * columns, bytes_accessed=2 * width * (inside + 3 * columns), transcendentals=0
        ),
    )(*blocks, cot, right_wide, left3, error)


def finish_kernel(steps, first_ref, second_ref, one_ref, two_ref, cot_ref, out_ref):
    step = pl.program_id(0)

    @pl.when(step < steps)
    def _():
        out_ref[...] = (one_ref[...] + dot(first_ref[...], cot_ref[...], ((0,), (0,)))).astype(BF16)

    @pl.when(step >= steps)
    def _():
        out_ref[...] = (two_ref[...] + dot(second_ref[...], cot_ref[...], ((0,), (0,)))).astype(BF16)


def finish(first, second, one, two, cot):
    depth, width = first.shape
    columns = cot.shape[1]
    steps = width // LAST
    low = lambda i: jnp.minimum(i, steps - 1)
    high = lambda i: jnp.maximum(i - steps, 0)
    return pl.pallas_call(
        lambda *refs: finish_kernel(steps, *refs),
        grid=(2 * steps,),
        in_specs=[
            pl.BlockSpec((depth, LAST), lambda i: (0, low(i))),
            pl.BlockSpec((depth, LAST), lambda i: (0, high(i))),
            pl.BlockSpec((LAST, columns), lambda i: (low(i), 0)),
            pl.BlockSpec((LAST, columns), lambda i: (high(i), 0)),
            pl.BlockSpec((depth, columns), lambda i: (0, 0)),
        ],
        out_specs=pl.BlockSpec((LAST, columns), lambda i: (i, 0)),
        out_shape=jax.ShapeDtypeStruct((2 * width, columns), BF16),
        compiler_params=pltpu.CompilerParams(vmem_limit_bytes=24 << 20),
        cost_estimate=pl.CostEstimate(
            flops=4 * depth * width * columns, bytes_accessed=4 * width * (depth + 3 * columns), transcendentals=0
        ),
    )(first, second, one, two, cot)


def spread(x, axis):
    return jnp.broadcast_to(x, (lax.axis_size(axis),) + x.shape)


def shards(tokens, cotangent, error_buffer, start_basis):
    highest = lax.Precision.HIGHEST
    tokens, cot, error = tokens[0], cotangent[0], error_buffer[0]
    planes = lax.axis_size("tensor")
    replicas = lax.axis_size("dp")
    depth, d = tokens.shape
    columns, rank = start_basis.shape
    width = d // CHUNKS
    ring = Ring([tokens[:, c * width : (c + 1) * width] for c in range(CHUNKS)], "tensor")

    start3 = split_rows(after(start_basis, *ring.up).T)
    weights = join_rows(dot(start3, cot, ((1,), (1,))))
    weights = weights.reshape(rank, planes, depth).transpose(1, 0, 2)
    moved = [ring.step(weights)]
    moved.append(ring.step(weights))
    weight = jnp.sum(lax.all_to_all(weights, "tensor", 0, 0), axis=0)
    left_part = join_rows(dot(split_rows(weight), tokens, ((1,), (0,))) + dot(start3, error, ((1,), (1,))))
    height = d // replicas
    left_part = left_part.reshape(rank, replicas, height).transpose(1, 0, 2)
    left_rows = after(jnp.sum(lax.all_to_all(left_part, "dp", 0, 0), axis=0), *moved[0])
    left_rows = spread(left_rows, "tensor")
    moved.append(ring.step(left_rows))
    moved.append(ring.step(left_rows))
    whole_rows = after(jnp.sum(lax.all_to_all(left_rows, "tensor", 0, 0), axis=0), *moved[1])
    left = lax.all_to_all(spread(whole_rows, "dp"), "dp", 0, 0)
    left = after(left.transpose(1, 0, 2).reshape(rank, d), *moved[2])

    left3 = split_rows(left)
    inner = spread(join_rows(dot(left3, tokens, ((1,), (1,)))), "tensor")
    moved.append(ring.step(inner))
    moved.append(ring.step(inner))
    moved.append(ring.step(inner))
    inner = lax.all_to_all(inner, "tensor", 0, 0).transpose(1, 0, 2).reshape(rank, planes * depth)
    inner = after(inner, *moved[3])
    right_part = join_rows(dot(split_rows(inner), cot, ((1,), (0,))) + dot(left3, error, ((1,), (0,))))
    right_part = spread(right_part, "dp")
    parts = after(lax.all_to_all(right_part, "dp", 0, 0), *moved[4])
    answer, right_wide = solve(left3, parts)
    blocks = ring.blocks

    mine = lax.dynamic_slice_in_dim(left, lax.axis_index("dp") * height, height, 1)
    decompressed = lax.dot_general(
        mine, answer, (((0,), (0,)), ((), ())), precision=highest, preferred_element_type=F32
    ).astype(BF16)

    half = planes // 2
    place = lax.axis_index("tensor") * depth
    turned = lax.dynamic_slice_in_dim(jnp.concatenate([cot, cot], axis=0), place, planes * depth, 0)
    early = jnp.concatenate([turned[: half * depth], turned[(half + 1) * depth :]], axis=0)
    parts = [
        partial(c * width, blocks[c][:half] + blocks[c][half + 1 :], early, right_wide, left3, error)
        for c in range(CHUNKS)
    ]
    out = finish(blocks[0][half], blocks[1][half], *parts, turned[half * depth : (half + 1) * depth])
    return decompressed, out[None]


def solution(mesh):
    in_specs = (
        P("dp", "tensor", None),
        P("dp", None, "tensor"),
        P("dp", None, "tensor"),
        P("tensor", None),
    )
    out_specs = (P("dp", "tensor"), P("dp", None, "tensor"))
    return jax.shard_map(shards, mesh=mesh, in_specs=in_specs, out_specs=out_specs, check_vma=False)
```

time: 644 us -> 193 us (0.30)
  waiting for transfers between devices: 432 us -> 74.8 us
  blocking collectives: 123 us -> 0 us
  starting transfers between devices: 0.08 us -> 62.2 us
  matrix products: 50.3 us -> 11.2 us
  Pallas kernels: 0 us -> 22.4 us
  between operations: 14.1 us -> 1.1 us
  other arithmetic: 15.8 us -> 5.33 us
  local copies, waits for them, and re-layouts: 4.92 us -> 12.4 us
    psum x1 -> x0, waiting for transfers between devices: 253 us -> none  [shards(): left_factor = lax.psum(left_part, ('dp', 'tensor'))]
    all_gather x1 -> x0, waiting for transfers between devices: 178 us -> none  [shards(): lax.all_gather(local_tokens, 'tensor', axis=0, tiled=True)]
    psum x1 -> x0, blocking collectives: 123 us -> none  [shards(): right_factor = lax.psum(right_part, 'dp')]
    all_to_all x0 -> x6, waiting for transfers between devices: none -> 46.4 us  [the longest x1 15.4 us: shards(): lax.all_to_all(left_part, 'dp', 0, 0)]
    all_to_all x0 -> x6, starting transfers between devices: none -> 46.4 us  [the longest x1 10.3 us: shards(): left = lax.all_to_all(spread(whole_rows, 'dp'), 'dp', 0, 0)]
    dot_general x5 -> x7, matrix products: 48.1 us -> 11.2 us  [the longest x6 9.37 us: dot(): return lax.dot_general(a, b, (dims, ((), ())), preferred_element_type=F32)]
    ppermute x0 -> x14, waiting for transfers between devices: none -> 28.4 us  [shift(): return lax.ppermute(x, axis, [(j, (j + by) % size) for j in range(size)])]
    pallas_call x0 -> x4, Pallas kernels: none -> 22.4 us  [the longest x2 11.3 us: partial(): pl.pallas_call(lambda *refs: partial_kernel(count, *refs), grid=(width //...]
  transfers between devices with their start and end apart: 2 -> 20, of which waited for: 2 -> 9; matrix products, arithmetic and copies ran while one was open for 0% -> 12% of each run, Pallas kernels for 0% -> 9%
where the time goes in v2:
time: 193 us; the launch traced here: 189 us
  waiting for transfers between devices  74.8 us (39%)
  starting transfers between devices  62.2 us (32%)
  Pallas kernels  22.4 us (12%)
  local copies, waits for them, and re-layouts  12.4 us (6%)
  matrix products  11.2 us (6%)
  other arithmetic  5.33 us (3%)
    ppermute x14, waiting for transfers between devices, shift(): return lax.ppermute(x, axis, [(j, (j + by) % size) for j in range(size)])  28.4 us
    ppermute x14, starting transfers between devices, shift(): return lax.ppermute(x, axis, [(j, (j + by) % size) for j in range(size)])  15.8 us
    all_to_all x1, waiting for transfers between devices, shards(): lax.all_to_all(left_part, 'dp', 0, 0)  15.4 us
    all_to_all x1, waiting for transfers between devices, shards(): left = lax.all_to_all(spread(whole_rows, 'dp'), 'dp', 0, 0)  14.2 us
    pallas_call x2, Pallas kernels, partial(): pl.pallas_call(lambda *refs: partial_kernel(count, *refs), grid=(width //...  11.3 us
    all_to_all x1, starting transfers between devices, shards(): left = lax.all_to_all(spread(whole_rows, 'dp'), 'dp', 0, 0)  10.3 us
    all_to_all x1, starting transfers between devices, shards(): lax.all_to_all(left_part, 'dp', 0, 0)  10.1 us
    all_to_all x1, starting transfers between devices, shards(): parts = after(lax.all_to_all(right_part, 'dp', 0, 0), *moved[4])  10 us
  transfers between devices with their start and end apart: 20, of which 9 were waited for; matrix products, arithmetic and copies ran while one was open for 12% of the time, Pallas kernels for 9%

profile of v2, /device:TPU:1, one launch (start us, length us, event | category | flops | bytes accessed | tf_op | source)
XLA Modules:
  0.0 189.5 jit_solution(13391041461132934340)
XLA Ops:
  0.7 1.7 fusion.32
  2.7 0.7 bitcast_bitcast_fusion.1
  3.5 9.0 %all-to-all-start = ((f32[8,32,128]{2,1,0:T(8,128)}), f32[8,32,128]{2,1,0:T(8,128)S(1)}, u32[]{:S(2)}, u32[]{:S(2)}) async-start(f32[8,32,128]{2,1,0:T(8,128)} %bitcast_bitcast_fusion.1), calls=%async_computation | async-start | bytes 262144 | tf_op jit(solution)/shard_map/all_to_all | solution.py:198
  12.5 2.7 %collective-permute-start.1 = (bf16[128,4096]{1,0:T(8,128)(2,1)S(1)}, bf16[128,4096]{1,0:T(8,128)(2,1)}, u32[]{:S(2)}, u32[]{:S(2)}) collective-permute-start(bf16[128,4096]{1,0:T(8,128)(2,1)S(1)} %get-tuple-element.23.refs_0_), channel_id=1, source_target_pairs={{0,7},{1,0},{2,1},{3,2},{4,3},{5,4},{6,5},{7,6},{8,15},{9,8},{10,9... | collective-permute-start | bytes 3145736 | tf_op jit(solution)/shard_map/ppermute | solution.py:37
  15.1 5.1 %all-to-all-done = f32[8,32,128]{2,1,0:T(8,128)S(1)} async-done(((f32[8,32,128]{2,1,0:T(8,128)}), f32[8,32,128]{2,1,0:T(8,128)S(1)}, u32[]{:S(2)}, u32[]{:S(2)}) %all-to-all-start) | async-done | bytes 131104 | tf_op jit(solution)/shard_map/all_to_all | solution.py:198
  20.3 2.3 %fusion.12 = f32[96,8192]{1,0:T(8,128)S(1)} fusion(bf16[32,128]{1,0:T(8,128)(2,1)S(1)} %get-tuple-element.54, bf16[32,128]{1,0:T(8,128)(2,1)S(1)} %get-tuple-element.55, bf16[32,128]{1,0:T(8,128)(2,1)S(1)} %get-tuple-element.53, bf16[1,128,8192]{2,1,0:T(8,128)(2,1)} %param.4), kind=kOutput, calls=%fused_computation.41 | convolution fusion | flops 201400320 | bytes 5267456 | tf_op jit(solution)/shard_map/dot_general | solution.py:32
  23.1 1.4 convolution_add_fusion
  24.6 1.1 copy.21
  25.7 10.1 %all-to-all-start.1 = ((f32[32,32,256]{2,1,0:T(8,128)}), f32[32,32,256]{2,1,0:T(8,128)}, u32[]{:S(2)}, u32[]{:S(2)}) async-start(f32[32,32,256]{2,1,0:T(8,128)} %bitcast.53), calls=%async_computation.1 | async-start | bytes 2097152 | tf_op jit(solution)/shard_map/all_to_all | solution.py:202
  36.3 1.1 collective-permute-start.2
  37.4 15.4 %all-to-all-done.1 = f32[32,32,256]{2,1,0:T(8,128)} async-done(((f32[32,32,256]{2,1,0:T(8,128)}), f32[32,32,256]{2,1,0:T(8,128)}, u32[]{:S(2)}, u32[]{:S(2)}) %all-to-all-start.1) | async-done | bytes 1048608 | tf_op jit(solution)/shard_map/all_to_all | solution.py:202
  52.8 1.3 reduce_sum.28
  54.1 0.7 broadcast_in_dim.15
  54.9 3.4 %all-to-all-start.2 = ((f32[8,32,256]{2,1,0:T(8,128)}), f32[8,32,256]{2,1,0:T(8,128)S(1)}, u32[]{:S(2)}, u32[]{:S(2)}) async-start(f32[8,32,256]{2,1,0:T(8,128)} %broadcast_in_dim.15), calls=%async_computation.2 | async-start | bytes 524288 | tf_op jit(solution)/shard_map/all_to_all | solution.py:206
  58.3 1.4 collective-permute-start.4
  59.6 1.4 collective-permute-start.5
  61.0 9.4 %all-to-all-done.2 = f32[8,32,256]{2,1,0:T(8,128)S(1)} async-done(((f32[8,32,256]{2,1,0:T(8,128)}), f32[8,32,256]{2,1,0:T(8,128)S(1)}, u32[]{:S(2)}, u32[]{:S(2)}) %all-to-all-start.2) | async-done | bytes 262176 | tf_op jit(solution)/shard_map/all_to_all | solution.py:206
  70.5 1.1 broadcast_in_dim.16
  71.5 10.3 %all-to-all-start.3 = ((f32[32,32,256]{2,1,0:T(8,128)}), f32[32,32,256]{2,1,0:T(8,128)}, u32[]{:S(2)}, u32[]{:S(2)}) async-start(f32[32,32,256]{2,1,0:T(8,128)} %broadcast_in_dim.16), calls=%async_computation.3 | async-start | bytes 2097152 | tf_op jit(solution)/shard_map/all_to_all | solution.py:207
  81.9 0.6 collective-permute-start.6
  82.5 2.2 %collective-permute-start.7 = (bf16[128,4096]{1,0:T(8,128)(2,1)}, bf16[128,4096]{1,0:T(8,128)(2,1)}, u32[]{:S(2)}, u32[]{:S(2)}) collective-permute-start(bf16[128,4096]{1,0:T(8,128)(2,1)} %collective-permute-done.3.refs_1_), channel_id=1, source_target_pairs={{0,7},{1,0},{2,1},{3,2},{4,3},{5,4},{6,5},{7,6},{8,15},{9,8},{10,9... | collective-permute-start | bytes 3145736 | tf_op jit(solution)/shard_map/ppermute | solution.py:37
  84.6 14.2 %all-to-all-done.3 = f32[32,32,256]{2,1,0:T(8,128)} async-done(((f32[32,32,256]{2,1,0:T(8,128)}), f32[32,32,256]{2,1,0:T(8,128)}, u32[]{:S(2)}, u32[]{:S(2)}) %all-to-all-start.3) | async-done | bytes 1048608 | tf_op jit(solution)/shard_map/all_to_all | solution.py:207
  98.8 1.5 copy.16
  100.3 1.0 copy-done.7
  101.5 0.8 fusion.29
  102.5 0.7 broadcast_in_dim.17
  103.1 3.6 %all-to-all-start.4 = ((f32[8,32,128]{2,1,0:T(8,128)}), f32[8,32,128]{2,1,0:T(8,128)S(1)}, u32[]{:S(2)}, u32[]{:S(2)}) async-start(f32[8,32,128]{2,1,0:T(8,128)} %broadcast_in_dim.17), calls=%async_computation.4 | async-start | bytes 262144 | tf_op jit(solution)/shard_map/all_to_all | solution.py:215
  106.7 1.4 fusion.1
  108.1 0.7 slice.83
  108.8 3.7 %collective-permute-done.7.refs_2_ = bf16[128,4096]{1,0:T(8,128)(2,1)} collective-permute-done((bf16[128,4096]{1,0:T(8,128)(2,1)}, bf16[128,4096]{1,0:T(8,128)(2,1)}, u32[]{:S(2)}, u32[]{:S(2)}) %collective-permute-start.7) | collective-permute-done | bytes 1048608 | tf_op jit(solution)/shard_map/ppermute | solution.py:37
  112.6 1.2 collective-permute-start.8
  113.8 1.5 collective-permute-start.9
  115.2 1.1 collective-permute-start.11
  116.3 2.3 %all-to-all-done.4 = f32[8,32,128]{2,1,0:T(8,128)S(1)} async-done(((f32[8,32,128]{2,1,0:T(8,128)}), f32[8,32,128]{2,1,0:T(8,128)S(1)}, u32[]{:S(2)}, u32[]{:S(2)}) %all-to-all-start.4) | async-done | bytes 131104 | tf_op jit(solution)/shard_map/all_to_all | solution.py:215
  118.7 1.3 fusion.2
  120.0 3.3 %convolution_add_fusion.1 = f32[96,256]{1,0:T(8,128)S(1)} fusion(f32[96,256]{1,0:T(8,128)S(1)} %fusion.2, bf16[1,8192,256]{2,1,0:T(8,128)(2,1)} %param.6, bf16[32,8192]{1,0:T(8,128)(2,1)} %copy-done.9, bf16[32,8192]{1,0:T(8,128)(2,1)} %copy-done.10, bf16[32,8192]{1,0:T(8,128)(2,1)S(1)} %get-tuple-element.44), kind=kOutput, calls=%fused_computation.7 | convolution fusion | flops 407396352 | bytes 5963776 | tf_op jit(solution)/shard_map/dot_general | solution.py:32
  123.3 1.1 broadcast_in_dim.18
  124.4 10.0 %all-to-all-start.5 = ((f32[32,32,256]{2,1,0:T(8,128)}), f32[32,32,256]{2,1,0:T(8,128)}, u32[]{:S(2)}, u32[]{:S(2)}) async-start(f32[32,32,256]{2,1,0:T(8,128)} %broadcast_in_dim.18), calls=%async_computation.5 | async-start | bytes 2097152 | tf_op jit(solution)/shard_map/all_to_all | solution.py:219
  134.6 4.8 %collective-permute-done.8.refs_4_ = bf16[128,4096]{1,0:T(8,128)(2,1)} collective-permute-done((bf16[128,4096]{1,0:T(8,128)(2,1)S(1)}, bf16[128,4096]{1,0:T(8,128)(2,1)}, u32[]{:S(2)}, u32[]{:S(2)}) %collective-permute-start.8) | collective-permute-done | bytes 1048608 | tf_op jit(solution)/shard_map/ppermute | solution.py:37
  139.4 19.3 %collective-permute-done.11.refs_3_ = bf16[128,4096]{1,0:T(8,128)(2,1)} collective-permute-done((bf16[128,4096]{1,0:T(8,128)(2,1)}, bf16[128,4096]{1,0:T(8,128)(2,1)}, u32[]{:S(2)}, u32[]{:S(2)}) %collective-permute-start.11) | collective-permute-done | bytes 1048608 | tf_op jit(solution)/shard_map/ppermute | solution.py:37
  158.7 2.2 %collective-permute-start.12 = (bf16[128,4096]{1,0:T(8,128)(2,1)}, bf16[128,4096]{1,0:T(8,128)(2,1)}, u32[]{:S(2)}, u32[]{:S(2)}) collective-permute-start(bf16[128,4096]{1,0:T(8,128)(2,1)} %collective-permute-done.11.refs_3_), channel_id=1, source_target_pairs={{0,7},{1,0},{2,1},{3,2},{4,3},{5,4},{6,5},{7,6},{8,15},{9,8},{10,9... | collective-permute-start | bytes 3145736 | tf_op jit(solution)/shard_map/ppermute | solution.py:37
  160.9 1.5 pad_maximum_fusion.left_ref.refs_9_
  162.4 6.0 %shard_map.59 = (f32[32,256]{1,0:T(8,128)S(1)}, bf16[192,256]{1,0:T(8,128)(2,1)S(1)}) custom-call(bf16[96,8192]{1,0:T(8,128)(2,1)S(1)} %pad_maximum_fusion.left_ref.refs_9_, f32[32,32,256]{2,1,0:T(8,128)} %all-to-all-done.5.parts_ref), custom_call_target="tpu_custom_call" | custom-call | flops 16777216 | bytes 3145728 | tf_op jit(solution)/shard_map/pallas_call | solution.py:96
  168.5 2.2 %copy-done.1 = bf16[1,8192,256]{2,1,0:T(8,128)(2,1)S(1)} copy-done((bf16[1,8192,256]{2,1,0:T(8,128)(2,1)S(1)}, bf16[1,8192,256]{2,1,0:T(8,128)(2,1)}, u32[]{:S(2)}) %copy-start.1) | copy-done | bytes 4194328
  170.7 5.5 %shard_map.60.refs_2_ = f32[4096,256]{1,0:T(8,128)S(1)} custom-call(bf16[128,4096]{1,0:T(8,128)(2,1)S(1)} %copy-done.3, bf16[128,4096]{1,0:T(8,128)(2,1)} %collective-permute-done.1.refs_1_, bf16[128,4096]{1,0:T(8,128)(2,1)} %collective-permute-done.5.refs_2_, bf16[128,4096]{1,0:T(8,128)(2,1)} %collective-permute-done.9.refs_3_, ...), custom_call_target="tpu_custom_call" | custom-call | flops 1879048192 | bytes 13631488 | tf_op jit(solution)/shard_map/pallas_call | solution.py:123
  176.2 5.7 %shard_map.61.refs_3_ = f32[4096,256]{1,0:T(8,128)S(1)} custom-call(bf16[128,4096]{1,0:T(8,128)(2,1)S(1)} %get-tuple-element.25.refs_0_, bf16[128,4096]{1,0:T(8,128)(2,1)} %collective-permute-done.3.refs_1_, bf16[128,4096]{1,0:T(8,128)(2,1)} %collective-permute-done.7.refs_2_, bf16[128,4096]{1,0:T(8,128)(2,1)} %collective-permute-done.11.refs_3_, ...), custom_call_target="tpu_custom_call" | custom-call | flops 1879048192 | bytes 13631488 | tf_op jit(solution)/shard_map/pallas_call | solution.py:123
  182.0 1.8 convolution_convert_fusion
  184.3 5.1 %shard_map.62 = bf16[8192,256]{1,0:T(8,128)(2,1)} custom-call(bf16[128,4096]{1,0:T(8,128)(2,1)} %collective-permute-done.10.refs_0_, bf16[128,4096]{1,0:T(8,128)(2,1)} %collective-permute-done.12.refs_1_, f32[4096,256]{1,0:T(8,128)S(1)} %shard_map.60.refs_2_, f32[4096,256]{1,0:T(8,128)S(1)} %shard_map.61.refs_3_, bf16[128,256]{1,0:T(8,128)(2,1)S(1)} %slice.84.refs_4_), custom_call_target="tpu_custom_call" | custom-call | flops 536870912 | bytes 14680064 | tf_op jit(solution)/shard_map/pallas_call | solution.py:160
  (56 shorter events, 2.5 us)
Async XLA Ops:
  0.6 1.8 copy-start.13
  0.6 1.8 copy-start.11
  2.4 20.2 %copy-start.2 = (bf16[128,4096]{1,0:T(8,128)(2,1)}, bf16[128,4096]{1,0:T(8,128)(2,1)S(1)}, u32[]{:S(2)}) copy-start(bf16[128,4096]{1,0:T(8,128)(2,1)S(1)} %get-tuple-element.23.refs_0_) | copy-start | bytes 3145732
  3.5 16.8 %all-to-all-start = ((f32[8,32,128]{2,1,0:T(8,128)}), f32[8,32,128]{2,1,0:T(8,128)S(1)}, u32[]{:S(2)}, u32[]{:S(2)}) async-start(f32[8,32,128]{2,1,0:T(8,128)} %bitcast_bitcast_fusion.1), calls=%async_computation | async-start | bytes 262144 | tf_op jit(solution)/shard_map/all_to_all | solution.py:198
  12.5 41.6 %collective-permute-start.1 = (bf16[128,4096]{1,0:T(8,128)(2,1)S(1)}, bf16[128,4096]{1,0:T(8,128)(2,1)}, u32[]{:S(2)}, u32[]{:S(2)}) collective-permute-start(bf16[128,4096]{1,0:T(8,128)(2,1)S(1)} %get-tuple-element.23.refs_0_), channel_id=1, source_target_pairs={{0,7},{1,0},{2,1},{3,2},{4,3},{5,4},{6,5},{7,6},{8,15},{9,8},{10,9... | collective-permute-start | bytes 3145736 | tf_op jit(solution)/shard_map/ppermute | solution.py:37
  15.1 39.0 %collective-permute-start = (bf16[128,4096]{1,0:T(8,128)(2,1)S(1)}, bf16[128,4096]{1,0:T(8,128)(2,1)}, u32[]{:S(2)}, u32[]{:S(2)}) collective-permute-start(bf16[128,4096]{1,0:T(8,128)(2,1)S(1)} %get-tuple-element.23.refs_0_), channel_id=1, source_target_pairs={{0,1},{1,2},{2,3},{3,4},{4,5},{5,6},{6,7},{7,0},{8,9},{9,10},{10,1... | collective-permute-start | bytes 3145736 | tf_op jit(solution)/shard_map/ppermute | solution.py:37
  20.3 2.8 %copy-start = (bf16[1,8192,256]{2,1,0:T(8,128)(2,1)S(1)}, bf16[1,8192,256]{2,1,0:T(8,128)(2,1)}, u32[]{:S(2)}) copy-start(bf16[1,8192,256]{2,1,0:T(8,128)(2,1)} %param.6) | copy-start | bytes 12582916
  25.7 27.1 %all-to-all-start.1 = ((f32[32,32,256]{2,1,0:T(8,128)}), f32[32,32,256]{2,1,0:T(8,128)}, u32[]{:S(2)}, u32[]{:S(2)}) async-start(f32[32,32,256]{2,1,0:T(8,128)} %bitcast.53), calls=%async_computation.1 | async-start | bytes 2097152 | tf_op jit(solution)/shard_map/all_to_all | solution.py:202
  35.9 34.6 %collective-permute-start.3 = (bf16[128,4096]{1,0:T(8,128)(2,1)S(1)}, bf16[128,4096]{1,0:T(8,128)(2,1)}, u32[]{:S(2)}, u32[]{:S(2)}) collective-permute-start(bf16[128,4096]{1,0:T(8,128)(2,1)S(1)} %get-tuple-element.25.refs_0_), channel_id=1, source_target_pairs={{0,7},{1,0},{2,1},{3,2},{4,3},{5,4},{6,5},{7,6},{8,15},{9,8},{10,9... | collective-permute-start | bytes 3145736 | tf_op jit(solution)/shard_map/ppermute | solution.py:37
  36.3 34.2 %collective-permute-start.2 = (bf16[128,4096]{1,0:T(8,128)(2,1)S(1)}, bf16[128,4096]{1,0:T(8,128)(2,1)}, u32[]{:S(2)}, u32[]{:S(2)}) collective-permute-start(bf16[128,4096]{1,0:T(8,128)(2,1)S(1)} %get-tuple-element.25.refs_0_), channel_id=1, source_target_pairs={{0,1},{1,2},{2,3},{3,4},{4,5},{5,6},{6,7},{7,0},{8,9},{9,10},{10,1... | collective-permute-start | bytes 3145736 | tf_op jit(solution)/shard_map/ppermute | solution.py:37
  54.9 15.6 %all-to-all-start.2 = ((f32[8,32,256]{2,1,0:T(8,128)}), f32[8,32,256]{2,1,0:T(8,128)S(1)}, u32[]{:S(2)}, u32[]{:S(2)}) async-start(f32[8,32,256]{2,1,0:T(8,128)} %broadcast_in_dim.15), calls=%async_computation.2 | async-start | bytes 524288 | tf_op jit(solution)/shard_map/all_to_all | solution.py:206
  58.3 42.0 %collective-permute-start.4 = (bf16[128,4096]{1,0:T(8,128)(2,1)}, bf16[128,4096]{1,0:T(8,128)(2,1)S(1)}, u32[]{:S(2)}, u32[]{:S(2)}) collective-permute-start(bf16[128,4096]{1,0:T(8,128)(2,1)} %collective-permute-done.refs_6_), channel_id=1, source_target_pairs={{0,1},{1,2},{2,3},{3,4},{4,5},{5,6},{6,7},{7,0},{8,9},{9,10},{10,1... | collective-permute-start | bytes 3145736 | tf_op jit(solution)/shard_map/ppermute | solution.py:37
  59.6 40.7 %collective-permute-start.5 = (bf16[128,4096]{1,0:T(8,128)(2,1)}, bf16[128,4096]{1,0:T(8,128)(2,1)}, u32[]{:S(2)}, u32[]{:S(2)}) collective-permute-start(bf16[128,4096]{1,0:T(8,128)(2,1)} %collective-permute-done.1.refs_1_), channel_id=1, source_target_pairs={{0,7},{1,0},{2,1},{3,2},{4,3},{5,4},{6,5},{7,6},{8,15},{9,8},{10,9... | collective-permute-start | bytes 3145736 | tf_op jit(solution)/shard_map/ppermute | solution.py:37
  71.5 27.3 %all-to-all-start.3 = ((f32[32,32,256]{2,1,0:T(8,128)}), f32[32,32,256]{2,1,0:T(8,128)}, u32[]{:S(2)}, u32[]{:S(2)}) async-start(f32[32,32,256]{2,1,0:T(8,128)} %broadcast_in_dim.16), calls=%async_computation.3 | async-start | bytes 2097152 | tf_op jit(solution)/shard_map/all_to_all | solution.py:207
  81.9 36.8 %collective-permute-start.6 = (bf16[128,4096]{1,0:T(8,128)(2,1)}, bf16[128,4096]{1,0:T(8,128)(2,1)}, u32[]{:S(2)}, u32[]{:S(2)}) collective-permute-start(bf16[128,4096]{1,0:T(8,128)(2,1)} %collective-permute-done.2.refs_6_), channel_id=1, source_target_pairs={{0,1},{1,2},{2,3},{3,4},{4,5},{5,6},{6,7},{7,0},{8,9},{9,10},{10,1... | collective-permute-start | bytes 3145736 | tf_op jit(solution)/shard_map/ppermute | solution.py:37
  82.5 30.1 %collective-permute-start.7 = (bf16[128,4096]{1,0:T(8,128)(2,1)}, bf16[128,4096]{1,0:T(8,128)(2,1)}, u32[]{:S(2)}, u32[]{:S(2)}) collective-permute-start(bf16[128,4096]{1,0:T(8,128)(2,1)} %collective-permute-done.3.refs_1_), channel_id=1, source_target_pairs={{0,7},{1,0},{2,1},{3,2},{4,3},{5,4},{6,5},{7,6},{8,15},{9,8},{10,9... | collective-permute-start | bytes 3145736 | tf_op jit(solution)/shard_map/ppermute | solution.py:37
  98.8 2.7 %copy-start.6 = (bf16[1,128,8192]{2,1,0:T(8,128)(2,1)S(1)}, bf16[1,128,8192]{2,1,0:T(8,128)(2,1)}, u32[]{:S(2)}) copy-start(bf16[1,128,8192]{2,1,0:T(8,128)(2,1)} %param.4) | copy-start | bytes 6291460
  100.3 1.0 copy-start.7
  100.3 12.2 %copy-start.4 = (bf16[128,4096]{1,0:T(8,128)(2,1)}, bf16[128,4096]{1,0:T(8,128)(2,1)S(1)}, u32[]{:S(2)}) copy-start(bf16[128,4096]{1,0:T(8,128)(2,1)S(1)} %collective-permute-done.4.refs_5_) | copy-start | bytes 3145732
  101.5 0.8 copy-start.9
  101.5 1.0 copy-start.10
  101.5 18.5 %copy-start.8 = (bf16[32,8192]{1,0:T(8,128)(2,1)}, bf16[32,8192]{1,0:T(8,128)(2,1)S(1)}, u32[]{:S(2)}) copy-start(bf16[32,8192]{1,0:T(8,128)(2,1)S(1)} %get-tuple-element.44) | copy-start | bytes 1572868
  103.1 15.5 %all-to-all-start.4 = ((f32[8,32,128]{2,1,0:T(8,128)}), f32[8,32,128]{2,1,0:T(8,128)S(1)}, u32[]{:S(2)}, u32[]{:S(2)}) async-start(f32[8,32,128]{2,1,0:T(8,128)} %broadcast_in_dim.17), calls=%async_computation.4 | async-start | bytes 262144 | tf_op jit(solution)/shard_map/all_to_all | solution.py:215
  112.6 26.8 %collective-permute-start.8 = (bf16[128,4096]{1,0:T(8,128)(2,1)S(1)}, bf16[128,4096]{1,0:T(8,128)(2,1)}, u32[]{:S(2)}, u32[]{:S(2)}) collective-permute-start(bf16[128,4096]{1,0:T(8,128)(2,1)S(1)} %collective-permute-done.4.refs_5_), channel_id=1, source_target_pairs={{0,1},{1,2},{2,3},{3,4},{4,5},{5,6},{6,7},{7,0},{8,9},{9,10},{10,1... | collective-permute-start | bytes 3145736 | tf_op jit(solution)/shard_map/ppermute | solution.py:37
  113.8 48.6 %collective-permute-start.9 = (bf16[128,4096]{1,0:T(8,128)(2,1)}, bf16[128,4096]{1,0:T(8,128)(2,1)}, u32[]{:S(2)}, u32[]{:S(2)}) collective-permute-start(bf16[128,4096]{1,0:T(8,128)(2,1)} %collective-permute-done.5.refs_2_), channel_id=1, source_target_pairs={{0,7},{1,0},{2,1},{3,2},{4,3},{5,4},{6,5},{7,6},{8,15},{9,8},{10,9... | collective-permute-start | bytes 3145736 | tf_op jit(solution)/shard_map/ppermute | solution.py:37
  115.2 43.4 %collective-permute-start.11 = (bf16[128,4096]{1,0:T(8,128)(2,1)}, bf16[128,4096]{1,0:T(8,128)(2,1)}, u32[]{:S(2)}, u32[]{:S(2)}) collective-permute-start(bf16[128,4096]{1,0:T(8,128)(2,1)} %collective-permute-done.7.refs_2_), channel_id=1, source_target_pairs={{0,7},{1,0},{2,1},{3,2},{4,3},{5,4},{6,5},{7,6},{8,15},{9,8},{10,9... | collective-permute-start | bytes 3145736 | tf_op jit(solution)/shard_map/ppermute | solution.py:37
  123.3 11.1 %copy-start.12 = (bf16[384,256]{1,0:T(8,128)(2,1)S(1)}, bf16[384,256]{1,0:T(8,128)(2,1)}, u32[]{:S(2)}) copy-start(bf16[384,256]{1,0:T(8,128)(2,1)} %slice.83) | copy-start | bytes 589828
  124.4 38.0 %all-to-all-start.5 = ((f32[32,32,256]{2,1,0:T(8,128)}), f32[32,32,256]{2,1,0:T(8,128)}, u32[]{:S(2)}, u32[]{:S(2)}) async-start(f32[32,32,256]{2,1,0:T(8,128)} %broadcast_in_dim.18), calls=%async_computation.5 | async-start | bytes 2097152 | tf_op jit(solution)/shard_map/all_to_all | solution.py:219
  134.5 41.7 %collective-permute-start.13 = (bf16[128,4096]{1,0:T(8,128)(2,1)}, bf16[128,4096]{1,0:T(8,128)(2,1)}, u32[]{:S(2)}, u32[]{:S(2)}) collective-permute-start(bf16[128,4096]{1,0:T(8,128)(2,1)} %collective-permute-done.6.refs_5_), channel_id=1, source_target_pairs={{0,1},{1,2},{2,3},{3,4},{4,5},{5,6},{6,7},{7,0},{8,9},{9,10},{10,1... | collective-permute-start | bytes 3145736 | tf_op jit(solution)/shard_map/ppermute | solution.py:37
  139.4 44.9 %collective-permute-start.10 = (bf16[128,4096]{1,0:T(8,128)(2,1)}, bf16[128,4096]{1,0:T(8,128)(2,1)}, u32[]{:S(2)}, u32[]{:S(2)}) collective-permute-start(bf16[128,4096]{1,0:T(8,128)(2,1)} %collective-permute-done.8.refs_4_), channel_id=1, source_target_pairs={{0,1},{1,2},{2,3},{3,4},{4,5},{5,6},{6,7},{7,0},{8,9},{9,10},{10,1... | collective-permute-start | bytes 3145736 | tf_op jit(solution)/shard_map/ppermute | solution.py:37
  158.7 25.7 %collective-permute-start.12 = (bf16[128,4096]{1,0:T(8,128)(2,1)}, bf16[128,4096]{1,0:T(8,128)(2,1)}, u32[]{:S(2)}, u32[]{:S(2)}) collective-permute-start(bf16[128,4096]{1,0:T(8,128)(2,1)} %collective-permute-done.11.refs_3_), channel_id=1, source_target_pairs={{0,7},{1,0},{2,1},{3,2},{4,3},{5,4},{6,5},{7,6},{8,15},{9,8},{10,9... | collective-permute-start | bytes 3145736 | tf_op jit(solution)/shard_map/ppermute | solution.py:37
  162.4 6.0 %copy-start.3 = (bf16[128,4096]{1,0:T(8,128)(2,1)S(1)}, bf16[128,4096]{1,0:T(8,128)(2,1)}, u32[]{:S(2)}) copy-start(bf16[128,4096]{1,0:T(8,128)(2,1)} %copy-done.2) | copy-start | bytes 3145732
  162.4 6.0 %copy-start.5 = (bf16[128,4096]{1,0:T(8,128)(2,1)S(1)}, bf16[128,4096]{1,0:T(8,128)(2,1)}, u32[]{:S(2)}) copy-start(bf16[128,4096]{1,0:T(8,128)(2,1)} %copy-done.4) | copy-start | bytes 3145732
  168.5 2.2 %copy-start.1 = (bf16[1,8192,256]{2,1,0:T(8,128)(2,1)S(1)}, bf16[1,8192,256]{2,1,0:T(8,128)(2,1)}, u32[]{:S(2)}) copy-start(bf16[1,8192,256]{2,1,0:T(8,128)(2,1)} %param.6) | copy-start | bytes 12582916

commit v3 on v2

--- a/solution.py
+++ b/solution.py
@@ -62,8 +62,8 @@
         return first, second
 
 
-def solve_kernel(left_ref, parts_ref, answer_ref, wide_ref):
-    rank = parts_ref.shape[1]
+def factor_kernel(left_ref, inverse_ref):
+    rank = inverse_ref.shape[0]
     gram = jnp.zeros((rank, rank), F32)
     for k in (2, 1, 0):
         block = dot(left_ref[...], left_ref[k * rank : (k + 1) * rank, :], ((1,), (1,)))
@@ -77,12 +77,26 @@
         scaled = both[j : j + 1, :] / spread_column[j : j + 1, :]
         both = both - jnp.where(row > j, spread_column, 0.0) * scaled
     pivots = jnp.sum(jnp.where(row == column, both, 0.0), axis=1, keepdims=True)
-    inverse = both[:, rank:] * (1.0 / jnp.sqrt(pivots))
+    inverse_ref[...] = both[:, rank:] * (1.0 / jnp.sqrt(pivots))
+
+
+def factor(left3):
+    rank = left3.shape[0] // 3
+    return pl.pallas_call(
+        factor_kernel,
+        out_shape=jax.ShapeDtypeStruct((rank, rank), F32),
+        compiler_params=pltpu.CompilerParams(vmem_limit_bytes=8 << 20),
+        cost_estimate=pl.CostEstimate(flops=1 << 24, bytes_accessed=3 << 20, transcendentals=0),
+    )(left3)
+
+
+def solve_kernel(inverse_ref, parts_ref, mine_ref, product_ref, wide_ref):
+    exact = dict(precision=lax.Precision.HIGHEST, preferred_element_type=F32)
+    inverse = inverse_ref[...]
     total = jnp.sum(parts_ref[...], axis=0)
-    exact = dict(precision=lax.Precision.HIGHEST, preferred_element_type=F32)
     right = lax.dot_general(inverse, total, (((1,), (0,)), ((), ())), **exact)
     answer = lax.dot_general(inverse.T, right, (((1,), (0,)), ((), ())), **exact)
-    answer_ref[...] = answer
+    product_ref[...] = lax.dot_general(mine_ref[...].T, answer, (((1,), (0,)), ((), ())), **exact).astype(BF16)
     share = answer * (-1.0 / parts_ref.shape[0])
     high = share.astype(BF16)
     rest = share - high.astype(F32)
@@ -91,17 +105,17 @@
     wide_ref[...] = jnp.concatenate([high, high, middle, middle, high, low], axis=0)
 
 
-def solve(left3, parts):
+def solve(inverse, parts, mine):
     _, rank, columns = parts.shape
     return pl.pallas_call(
         solve_kernel,
         out_shape=(
-            jax.ShapeDtypeStruct((rank, columns), F32),
+            jax.ShapeDtypeStruct((mine.shape[1], columns), BF16),
             jax.ShapeDtypeStruct((6 * rank, columns), BF16),
         ),
-        compiler_params=pltpu.CompilerParams(vmem_limit_bytes=24 << 20),
-        cost_estimate=pl.CostEstimate(flops=1 << 24, bytes_accessed=3 << 20, transcendentals=0),
-    )(left3, parts)
+        compiler_params=pltpu.CompilerParams(vmem_limit_bytes=8 << 20),
+        cost_estimate=pl.CostEstimate(flops=1 << 24, bytes_accessed=1 << 20, transcendentals=0),
+    )(inverse, parts, mine)
 
 
 def partial_kernel(count, *refs):
@@ -139,19 +153,48 @@
     )(*blocks, cot, right_wide, left3, error)
 
 
-def finish_kernel(steps, first_ref, second_ref, one_ref, two_ref, cot_ref, out_ref):
+def early_kernel(count, *refs):
+    blocks, (cot_ref, error_ref), out_ref = refs[:count], refs[count : count + 2], refs[-1]
+    whole = jnp.concatenate([block[...] for block in blocks], axis=0)
+    out_ref[...] = dot(whole, cot_ref[...], ((0,), (0,))) + error_ref[...].astype(F32)
+
+
+def early_partial(start, blocks, cot, error):
+    count = len(blocks)
+    depth, width = blocks[0].shape
+    inside, columns = cot.shape
+    return pl.pallas_call(
+        lambda *refs: early_kernel(count, *refs),
+        grid=(width // TILE,),
+        in_specs=[pl.BlockSpec((depth, TILE), lambda i: (0, i)) for _ in range(count)]
+        + [
+            pl.BlockSpec((inside, columns), lambda i: (0, 0)),
+            pl.BlockSpec((TILE, columns), lambda i: (start // TILE + i, 0)),
+        ],
+        out_specs=pl.BlockSpec((TILE, columns), lambda i: (i, 0)),
+        out_shape=jax.ShapeDtypeStruct((width, columns), F32),
+        compiler_params=pltpu.CompilerParams(vmem_limit_bytes=48 << 20),
+        cost_estimate=pl.CostEstimate(flops=1 << 20, bytes_accessed=1 << 16, transcendentals=0),
+    )(*blocks, cot, error)
+
+
+def finish_kernel(steps, first_ref, second_ref, one_ref, two_ref, left_ref, right_ref, cot_ref, out_ref):
     step = pl.program_id(0)
 
     @pl.when(step < steps)
     def _():
-        out_ref[...] = (one_ref[...] + dot(first_ref[...], cot_ref[...], ((0,), (0,)))).astype(BF16)
+        rank = left_ref.shape[0] // 3
+        high, middle, low = (left_ref[k * rank : (k + 1) * rank, :] for k in range(3))
+        left = jnp.concatenate([high, middle, high, middle, low, high], axis=0)
+        product = dot(left, right_ref[...], ((0,), (0,)))
+        out_ref[...] = (one_ref[...] + dot(first_ref[...], cot_ref[...], ((0,), (0,))) + product).astype(BF16)
 
     @pl.when(step >= steps)
     def _():
         out_ref[...] = (two_ref[...] + dot(second_ref[...], cot_ref[...], ((0,), (0,)))).astype(BF16)
 
 
-def finish(first, second, one, two, cot):
+def finish(first, second, one, two, left3, right_wide, cot):
     depth, width = first.shape
     columns = cot.shape[1]
     steps = width // LAST
@@ -165,6 +208,8 @@
             pl.BlockSpec((depth, LAST), lambda i: (0, high(i))),
             pl.BlockSpec((LAST, columns), lambda i: (low(i), 0)),
             pl.BlockSpec((LAST, columns), lambda i: (high(i), 0)),
+            pl.BlockSpec((left3.shape[0], LAST), lambda i: (0, low(i))),
+            pl.BlockSpec(right_wide.shape, lambda i: (0, 0)),
             pl.BlockSpec((depth, columns), lambda i: (0, 0)),
         ],
         out_specs=pl.BlockSpec((LAST, columns), lambda i: (i, 0)),
@@ -173,7 +218,7 @@
         cost_estimate=pl.CostEstimate(
             flops=4 * depth * width * columns, bytes_accessed=4 * width * (depth + 3 * columns), transcendentals=0
         ),
-    )(first, second, one, two, cot)
+    )(first, second, one, two, left3, right_wide, cot)
 
 
 def spread(x, axis):
@@ -181,7 +226,6 @@
 
 
 def shards(tokens, cotangent, error_buffer, start_basis):
-    highest = lax.Precision.HIGHEST
     tokens, cot, error = tokens[0], cotangent[0], error_buffer[0]
     planes = lax.axis_size("tensor")
     replicas = lax.axis_size("dp")
@@ -190,50 +234,46 @@
     width = d // CHUNKS
     ring = Ring([tokens[:, c * width : (c + 1) * width] for c in range(CHUNKS)], "tensor")
 
-    start3 = split_rows(after(start_basis, *ring.up).T)
+    start3 = split_rows(start_basis.T)
     weights = join_rows(dot(start3, cot, ((1,), (1,))))
     weights = weights.reshape(rank, planes, depth).transpose(1, 0, 2)
-    moved = [ring.step(weights)]
+    moved = [ring.step()]
     moved.append(ring.step(weights))
-    weight = jnp.sum(lax.all_to_all(weights, "tensor", 0, 0), axis=0)
+    weight = after(jnp.sum(lax.all_to_all(weights, "tensor", 0, 0), axis=0), *moved[0])
+    moved.append(ring.step(weight))
     left_part = join_rows(dot(split_rows(weight), tokens, ((1,), (0,))) + dot(start3, error, ((1,), (1,))))
     height = d // replicas
     left_part = left_part.reshape(rank, replicas, height).transpose(1, 0, 2)
-    left_rows = after(jnp.sum(lax.all_to_all(left_part, "dp", 0, 0), axis=0), *moved[0])
+    left_rows = after(jnp.sum(lax.all_to_all(left_part, "dp", 0, 0), axis=0), *moved[1])
     left_rows = spread(left_rows, "tensor")
     moved.append(ring.step(left_rows))
-    moved.append(ring.step(left_rows))
-    whole_rows = after(jnp.sum(lax.all_to_all(left_rows, "tensor", 0, 0), axis=0), *moved[1])
-    left = lax.all_to_all(spread(whole_rows, "dp"), "dp", 0, 0)
-    left = after(left.transpose(1, 0, 2).reshape(rank, d), *moved[2])
-
-    left3 = split_rows(left)
-    inner = spread(join_rows(dot(left3, tokens, ((1,), (1,)))), "tensor")
-    moved.append(ring.step(inner))
-    moved.append(ring.step(inner))
-    moved.append(ring.step(inner))
-    inner = lax.all_to_all(inner, "tensor", 0, 0).transpose(1, 0, 2).reshape(rank, planes * depth)
-    inner = after(inner, *moved[3])
-    right_part = join_rows(dot(split_rows(inner), cot, ((1,), (0,))) + dot(left3, error, ((1,), (0,))))
-    right_part = spread(right_part, "dp")
-    parts = after(lax.all_to_all(right_part, "dp", 0, 0), *moved[4])
-    answer, right_wide = solve(left3, parts)
-    blocks = ring.blocks
-
-    mine = lax.dynamic_slice_in_dim(left, lax.axis_index("dp") * height, height, 1)
-    decompressed = lax.dot_general(
-        mine, answer, (((0,), (0,)), ((), ())), precision=highest, preferred_element_type=F32
-    ).astype(BF16)
-
+    whole_rows = after(jnp.sum(lax.all_to_all(left_rows, "tensor", 0, 0), axis=0), *moved[2])
+    moved.append(ring.step(whole_rows))
     half = planes // 2
     place = lax.axis_index("tensor") * depth
     turned = lax.dynamic_slice_in_dim(jnp.concatenate([cot, cot], axis=0), place, planes * depth, 0)
     early = jnp.concatenate([turned[: half * depth], turned[(half + 1) * depth :]], axis=0)
-    parts = [
-        partial(c * width, blocks[c][:half] + blocks[c][half + 1 :], early, right_wide, left3, error)
-        for c in range(CHUNKS)
-    ]
-    out = finish(blocks[0][half], blocks[1][half], *parts, turned[half * depth : (half + 1) * depth])
+    cot_last = turned[half * depth : (half + 1) * depth]
+    left = lax.all_to_all(spread(whole_rows, "dp"), "dp", 0, 0)
+    left = after(left.transpose(1, 0, 2).reshape(rank, d), early, cot_last, *moved[3])
+
+    left3 = split_rows(left)
+    mine = lax.dynamic_slice_in_dim(left, lax.axis_index("dp") * height, height, 1)
+    inner = spread(join_rows(dot(left3, tokens, ((1,), (1,)))), "tensor")
+    moved.append(ring.step(inner))
+    inverse = factor(after(left3, inner))
+    inner = lax.all_to_all(inner, "tensor", 0, 0).transpose(1, 0, 2).reshape(rank, planes * depth)
+    inner = after(inner, inverse, mine, *moved[4])
+    right_part = join_rows(dot(split_rows(inner), cot, ((1,), (0,))) + dot(left3, error, ((1,), (0,))))
+    right_part = spread(right_part, "dp")
+    moved.append(ring.step(right_part))
+    blocks = ring.blocks
+    one = early_partial(0, blocks[0][:half] + blocks[0][half + 1 :], early, error)
+    parts = after(lax.all_to_all(right_part, "dp", 0, 0), one, *moved[5])
+    decompressed, right_wide = solve(inverse, parts, mine)
+
+    two = partial(width, blocks[1][:half] + blocks[1][half + 1 :], early, right_wide, left3, error)
+    out = finish(blocks[0][half], blocks[1][half], one, two, left3, right_wide, cot_last)
     return decompressed, out[None]
 
 

time: 193 us -> 187 us (0.969); the launches traced: 189 us -> 186 us
  waiting for transfers between devices: 74.8 us -> 64.5 us
  starting transfers between devices: 62.2 us -> 68.3 us
  Pallas kernels: 22.4 us -> 25.4 us
    ppermute x14, waiting for transfers between devices: 28.4 us -> 3.29 us  [shift(): return lax.ppermute(x, axis, [(j, (j + by) % size) for j in range(size)])]
    all_to_all x2, waiting for transfers between devices: 5.1 us -> 21.3 us  [the longest x1 19.2 us: shards(): lax.all_to_all(weights, 'tensor', 0, 0)]
    pallas_call x1 -> x3, Pallas kernels: 6 us -> 13.8 us  [the longest x1 7.12 us: early_partial(): pl.pallas_call(lambda *refs: early_kernel(count, *refs), grid=(width // T...]
    ppermute x14, starting transfers between devices: 15.8 us -> 23.2 us  [shift(): return lax.ppermute(x, axis, [(j, (j + by) % size) for j in range(size)])]
    pallas_call x2 -> x1, Pallas kernels: 11.3 us -> 5.87 us  [partial(): pl.pallas_call(lambda *refs: partial_kernel(count, *refs), grid=(width //...]
    all_to_all x2, starting transfers between devices: 19 us -> 15.3 us  [the longest x1 11.2 us: shards(): parts = after(lax.all_to_all(right_part, 'dp', 0, 0), one, *moved[5])]
    unnamed x28 -> x24, local copies, waits for them, and re-layouts: 3.76 us -> 5.47 us
  transfers between devices with their start and end apart: 20 -> 20, of which waited for: 9 -> 8; matrix products, arithmetic and copies ran while one was open for 12% -> 10% of each run, Pallas kernels for 9% -> 11%
where the time goes in v3:
time: 187 us; the launch traced here: 186 us
  starting transfers between devices  68.3 us (37%)
  waiting for transfers between devices  64.5 us (34%)
  Pallas kernels  25.4 us (14%)
  local copies, waits for them, and re-layouts  12.8 us (7%)
  matrix products  9.52 us (5%)
  other arithmetic  4.1 us (2%)
    ppermute x14, starting transfers between devices, shift(): return lax.ppermute(x, axis, [(j, (j + by) % size) for j in range(size)])  23.2 us
    all_to_all x1, waiting for transfers between devices, shards(): lax.all_to_all(weights, 'tensor', 0, 0)  19.2 us
    all_to_all x1, waiting for transfers between devices, shards(): lax.all_to_all(left_part, 'dp', 0, 0)  15.4 us
    all_to_all x1, waiting for transfers between devices, shards(): left = lax.all_to_all(spread(whole_rows, 'dp'), 'dp', 0, 0)  12.7 us
    all_to_all x1, starting transfers between devices, shards(): left = lax.all_to_all(spread(whole_rows, 'dp'), 'dp', 0, 0)  11.8 us
    all_to_all x1, starting transfers between devices, shards(): parts = after(lax.all_to_all(right_part, 'dp', 0, 0), one, *moved[5])  11.2 us
    all_to_all x1, starting transfers between devices, shards(): lax.all_to_all(left_part, 'dp', 0, 0)  11.2 us
    dot_general x6, matrix products, dot(): return lax.dot_general(a, b, (dims, ((), ())), preferred_element_type=F32)  9.52 us
  transfers between devices with their start and end apart: 20, of which 8 were waited for; matrix products, arithmetic and copies ran while one was open for 10% of the time, Pallas kernels for 11%

profile of v3, /device:TPU:1, one launch (start us, length us, event | category | flops | bytes accessed | tf_op | source)
XLA Modules:
  0.0 185.7 jit_solution(10068660785185668856)
XLA Ops:
  0.7 1.8 fusion.30
  2.4 6.5 %collective-permute-start.1 = (bf16[128,4096]{1,0:T(8,128)(2,1)S(1)}, bf16[128,4096]{1,0:T(8,128)(2,1)}, u32[]{:S(2)}, u32[]{:S(2)}) collective-permute-start(bf16[128,4096]{1,0:T(8,128)(2,1)S(1)} %get-tuple-element.43.refs_0_), channel_id=1, source_target_pairs={{0,7},{1,0},{2,1},{3,2},{4,3},{5,4},{6,5},{7,6},{8,15},{9,8},{10,9... | collective-permute-start | bytes 3145736 | tf_op jit(solution)/shard_map/ppermute | solution.py:37
  9.2 0.7 bitcast_bitcast_fusion.1
  9.9 4.1 %all-to-all-start = ((f32[8,32,128]{2,1,0:T(8,128)}), f32[8,32,128]{2,1,0:T(8,128)S(1)}, u32[]{:S(2)}, u32[]{:S(2)}) async-start(f32[8,32,128]{2,1,0:T(8,128)} %bitcast_bitcast_fusion.1), calls=%async_computation | async-start | bytes 262144 | tf_op jit(solution)/shard_map/all_to_all | solution.py:242
  14.0 2.7 %collective-permute-start.3 = (bf16[128,4096]{1,0:T(8,128)(2,1)S(1)}, bf16[128,4096]{1,0:T(8,128)(2,1)}, u32[]{:S(2)}, u32[]{:S(2)}) collective-permute-start(bf16[128,4096]{1,0:T(8,128)(2,1)S(1)} %get-tuple-element.23.refs_0_), channel_id=1, source_target_pairs={{0,7},{1,0},{2,1},{3,2},{4,3},{5,4},{6,5},{7,6},{8,15},{9,8},{10,9... | collective-permute-start | bytes 3145736 | tf_op jit(solution)/shard_map/ppermute | solution.py:37
  16.7 19.2 %all-to-all-done = f32[8,32,128]{2,1,0:T(8,128)S(1)} async-done(((f32[8,32,128]{2,1,0:T(8,128)}), f32[8,32,128]{2,1,0:T(8,128)S(1)}, u32[]{:S(2)}, u32[]{:S(2)}) %all-to-all-start) | async-done | bytes 131104 | tf_op jit(solution)/shard_map/all_to_all | solution.py:242
  35.9 2.3 %fusion.11 = f32[96,8192]{1,0:T(8,128)S(1)} fusion(bf16[32,128]{1,0:T(8,128)(2,1)S(1)} %get-tuple-element.54, bf16[32,128]{1,0:T(8,128)(2,1)S(1)} %get-tuple-element.55, bf16[32,128]{1,0:T(8,128)(2,1)S(1)} %get-tuple-element.53, bf16[1,128,8192]{2,1,0:T(8,128)(2,1)} %param.4), kind=kOutput, calls=%fused_computation.39 | convolution fusion | flops 201400320 | bytes 5267456 | tf_op jit(solution)/shard_map/dot_general | solution.py:32
  38.7 1.4 convolution_add_fusion
  40.3 1.1 copy.21
  41.4 11.2 %all-to-all-start.1 = ((f32[32,32,256]{2,1,0:T(8,128)}), f32[32,32,256]{2,1,0:T(8,128)S(1)}, u32[]{:S(2)}, u32[]{:S(2)}) async-start(f32[32,32,256]{2,1,0:T(8,128)} %bitcast.45), calls=%async_computation.1 | async-start | bytes 2097152 | tf_op jit(solution)/shard_map/all_to_all | solution.py:247
  52.7 1.5 collective-permute-start.4
  54.1 15.4 %all-to-all-done.1 = f32[32,32,256]{2,1,0:T(8,128)S(1)} async-done(((f32[32,32,256]{2,1,0:T(8,128)}), f32[32,32,256]{2,1,0:T(8,128)S(1)}, u32[]{:S(2)}, u32[]{:S(2)}) %all-to-all-start.1) | async-done | bytes 1048608 | tf_op jit(solution)/shard_map/all_to_all | solution.py:247
  69.6 0.7 broadcast_in_dim.15
  70.3 3.4 %all-to-all-start.2 = ((f32[8,32,256]{2,1,0:T(8,128)}), f32[8,32,256]{2,1,0:T(8,128)S(1)}, u32[]{:S(2)}, u32[]{:S(2)}) async-start(f32[8,32,256]{2,1,0:T(8,128)} %broadcast_in_dim.15), calls=%async_computation.2 | async-start | bytes 524288 | tf_op jit(solution)/shard_map/all_to_all | solution.py:250
  73.7 1.4 collective-permute-start.6
  75.1 1.4 collective-permute-start.7
  76.5 9.5 %all-to-all-done.2 = f32[8,32,256]{2,1,0:T(8,128)S(1)} async-done(((f32[8,32,256]{2,1,0:T(8,128)}), f32[8,32,256]{2,1,0:T(8,128)S(1)}, u32[]{:S(2)}, u32[]{:S(2)}) %all-to-all-start.2) | async-done | bytes 262176 | tf_op jit(solution)/shard_map/all_to_all | solution.py:250
  86.0 1.1 broadcast_in_dim.16
  87.1 11.8 %all-to-all-start.3 = ((f32[32,32,256]{2,1,0:T(8,128)}), f32[32,32,256]{2,1,0:T(8,128)S(1)}, u32[]{:S(2)}, u32[]{:S(2)}) async-start(f32[32,32,256]{2,1,0:T(8,128)} %broadcast_in_dim.16), calls=%async_computation.3 | async-start | bytes 2097152 | tf_op jit(solution)/shard_map/all_to_all | solution.py:257
  98.9 1.4 fusion.1
  100.5 2.7 %collective-permute-start.9 = (bf16[128,4096]{1,0:T(8,128)(2,1)}, bf16[128,4096]{1,0:T(8,128)(2,1)}, u32[]{:S(2)}, u32[]{:S(2)}) collective-permute-start(bf16[128,4096]{1,0:T(8,128)(2,1)} %collective-permute-done.5.refs_2_), channel_id=1, source_target_pairs={{0,7},{1,0},{2,1},{3,2},{4,3},{5,4},{6,5},{7,6},{8,15},{9,8},{10,9... | collective-permute-start | bytes 3145736 | tf_op jit(solution)/shard_map/ppermute | solution.py:37
  103.1 12.7 %all-to-all-done.3 = f32[32,32,256]{2,1,0:T(8,128)S(1)} async-done(((f32[32,32,256]{2,1,0:T(8,128)}), f32[32,32,256]{2,1,0:T(8,128)S(1)}, u32[]{:S(2)}, u32[]{:S(2)}) %all-to-all-start.3) | async-done | bytes 1048608 | tf_op jit(solution)/shard_map/all_to_all | solution.py:257
  115.9 0.9 copy-done.6
  117.2 0.6 copy-done.5
  117.8 0.8 fusion.25
  118.6 0.7 broadcast_in_dim.17
  119.3 3.4 %all-to-all-start.4 = ((f32[8,32,128]{2,1,0:T(8,128)}), f32[8,32,128]{2,1,0:T(8,128)S(1)}, u32[]{:S(2)}, u32[]{:S(2)}) async-start(f32[8,32,128]{2,1,0:T(8,128)} %broadcast_in_dim.17), calls=%async_computation.4 | async-start | bytes 262144 | tf_op jit(solution)/shard_map/all_to_all | solution.py:265
  122.7 1.5 pad_maximum_fusion.left_ref.refs_9_.refs_4_
  124.1 1.4 collective-permute-start.10
  125.6 1.3 collective-permute-start.11
  126.9 4.1 %shard_map.59.inverse_ref = f32[32,32]{1,0:T(8,128)S(1)} custom-call(bf16[96,8192]{1,0:T(8,128)(2,1)S(1)} %pad_maximum_fusion.left_ref.refs_9_.refs_4_), custom_call_target="tpu_custom_call" | custom-call | flops 16777216 | bytes 3145728 | tf_op jit(solution)/shard_map/pallas_call | solution.py:85
  131.0 0.8 constant_dynamic-slice_fusion.mine_ref
  131.8 2.4 %all-to-all-done.4 = f32[8,32,128]{2,1,0:T(8,128)S(1)} async-done(((f32[8,32,128]{2,1,0:T(8,128)}), f32[8,32,128]{2,1,0:T(8,128)S(1)}, u32[]{:S(2)}, u32[]{:S(2)}) %all-to-all-start.4) | async-done | bytes 131104 | tf_op jit(solution)/shard_map/all_to_all | solution.py:265
  134.3 1.3 fusion.2
  135.5 3.5 %convolution_add_fusion.1 = f32[96,256]{1,0:T(8,128)S(1)} fusion(f32[96,256]{1,0:T(8,128)S(1)} %fusion.2, bf16[1,8192,256]{2,1,0:T(8,128)(2,1)} %param.6, bf16[32,8192]{1,0:T(8,128)(2,1)} %copy-done.8, bf16[32,8192]{1,0:T(8,128)(2,1)} %copy-done.9, bf16[32,8192]{1,0:T(8,128)(2,1)} %copy-done.7), kind=kOutput, calls=%fused_computation.6 | convolution fusion | flops 407396352 | bytes 5963776 | tf_op jit(solution)/shard_map/dot_general | solution.py:32
  139.0 1.1 broadcast_in_dim.18
  140.1 11.2 %all-to-all-start.5 = ((f32[32,32,256]{2,1,0:T(8,128)}), f32[32,32,256]{2,1,0:T(8,128)}, u32[]{:S(2)}, u32[]{:S(2)}) async-start(f32[32,32,256]{2,1,0:T(8,128)} %broadcast_in_dim.18), calls=%async_computation.5 | async-start | bytes 2097152 | tf_op jit(solution)/shard_map/all_to_all | solution.py:272
  151.4 0.8 collective-permute-start.12
  152.2 2.3 %collective-permute-done.11.refs_3_ = bf16[128,4096]{1,0:T(8,128)(2,1)} collective-permute-done((bf16[128,4096]{1,0:T(8,128)(2,1)}, bf16[128,4096]{1,0:T(8,128)(2,1)}, u32[]{:S(2)}, u32[]{:S(2)}) %collective-permute-start.11) | collective-permute-done | bytes 1048608 | tf_op jit(solution)/shard_map/ppermute | solution.py:37
  154.4 3.4 %collective-permute-start.13 = (bf16[128,4096]{1,0:T(8,128)(2,1)}, bf16[128,4096]{1,0:T(8,128)(2,1)}, u32[]{:S(2)}, u32[]{:S(2)}) collective-permute-start(bf16[128,4096]{1,0:T(8,128)(2,1)} %collective-permute-done.11.refs_3_), channel_id=1, source_target_pairs={{0,7},{1,0},{2,1},{3,2},{4,3},{5,4},{6,5},{7,6},{8,15},{9,8},{10,9... | collective-permute-start | bytes 3145736 | tf_op jit(solution)/shard_map/ppermute | solution.py:37
  157.9 1.2 copy-done.4
  159.1 7.1 %shard_map.60.refs_2_ = f32[4096,256]{1,0:T(8,128)} custom-call(bf16[128,4096]{1,0:T(8,128)(2,1)S(1)} %copy-done.4, bf16[128,4096]{1,0:T(8,128)(2,1)} %collective-permute-done.1.refs_1_, bf16[128,4096]{1,0:T(8,128)(2,1)} %collective-permute-done.5.refs_2_, bf16[128,4096]{1,0:T(8,128)(2,1)} %collective-permute-done.9.refs_3_, ...), custom_call_target="tpu_custom_call" | custom-call | flops 1048576 | bytes 65536 | tf_op jit(solution)/shard_map/pallas_call | solution.py:166
  166.2 2.1 %all-to-all-done.5.parts_ref = f32[32,32,256]{2,1,0:T(8,128)} async-done(((f32[32,32,256]{2,1,0:T(8,128)}), f32[32,32,256]{2,1,0:T(8,128)}, u32[]{:S(2)}, u32[]{:S(2)}) %all-to-all-start.5) | async-done | bytes 1048608 | tf_op jit(solution)/shard_map/all_to_all | solution.py:272
  168.3 2.6 %shard_map.61 = (bf16[256,256]{1,0:T(8,128)(2,1)}, bf16[192,256]{1,0:T(8,128)(2,1)S(1)}) custom-call(f32[32,32]{1,0:T(8,128)S(1)} %shard_map.59.inverse_ref, f32[32,32,256]{2,1,0:T(8,128)} %all-to-all-done.5.parts_ref, f32[32,256]{1,0:T(8,128)S(1)} %constant_dynamic-slice_fusion.mine_ref), custom_call_target="tpu_custom_call" | custom-call | flops 16777216 | bytes 1048576 | tf_op jit(solution)/shard_map/pallas_call | solution.py:110
  171.0 2.2 %copy-done.1 = bf16[1,8192,256]{2,1,0:T(8,128)(2,1)S(1)} copy-done((bf16[1,8192,256]{2,1,0:T(8,128)(2,1)S(1)}, bf16[1,8192,256]{2,1,0:T(8,128)(2,1)}, u32[]{:S(2)}) %copy-start.1) | copy-done | bytes 4194328
  173.2 5.9 %shard_map.62.refs_3_ = f32[4096,256]{1,0:T(8,128)S(1)} custom-call(bf16[128,4096]{1,0:T(8,128)(2,1)S(1)} %get-tuple-element.23.refs_0_, bf16[128,4096]{1,0:T(8,128)(2,1)} %collective-permute-done.3.refs_1_, bf16[128,4096]{1,0:T(8,128)(2,1)} %collective-permute-done.7.refs_2_, bf16[128,4096]{1,0:T(8,128)(2,1)} %collective-permute-done.11.refs_3_, ...), custom_call_target="tpu_custom_call" | custom-call | flops 1879048192 | bytes 13631488 | tf_op jit(solution)/shard_map/pallas_call | solution.py:137
  179.0 1.0 collective-permute-done.12.refs_0_
  180.0 5.7 %shard_map.63 = bf16[8192,256]{1,0:T(8,128)(2,1)} custom-call(bf16[128,4096]{1,0:T(8,128)(2,1)} %collective-permute-done.12.refs_0_, bf16[128,4096]{1,0:T(8,128)(2,1)} %collective-permute-done.13.refs_1_, f32[4096,256]{1,0:T(8,128)S(1)} %copy-done.2, f32[4096,256]{1,0:T(8,128)S(1)} %shard_map.62.refs_3_, ...), custom_call_target="tpu_custom_call" | custom-call | flops 536870912 | bytes 14680064 | tf_op jit(solution)/shard_map/pallas_call | solution.py:203
  (53 shorter events, 1.7 us)
Async XLA Ops:
  0.6 8.3 %copy-start.11 = (f32[256,32]{0,1:T(8,128)S(1)}, f32[256,32]{0,1:T(8,128)}, u32[]{:S(2)}) copy-start(f32[256,32]{0,1:T(8,128)} %param.7) | copy-start | bytes 98308
  0.6 8.3 %copy-start.10 = (bf16[1,1024,256]{2,1,0:T(8,128)(2,1)S(1)}, bf16[1,1024,256]{2,1,0:T(8,128)(2,1)}, u32[]{:S(2)}) copy-start(bf16[1,1024,256]{2,1,0:T(8,128)(2,1)} %param.5) | copy-start | bytes 1572868
  2.4 35.8 %copy-start.3 = (bf16[128,4096]{1,0:T(8,128)(2,1)}, bf16[128,4096]{1,0:T(8,128)(2,1)S(1)}, u32[]{:S(2)}) copy-start(bf16[128,4096]{1,0:T(8,128)(2,1)S(1)} %get-tuple-element.43.refs_0_) | copy-start | bytes 3145732
  2.4 33.5 %collective-permute-start.1 = (bf16[128,4096]{1,0:T(8,128)(2,1)S(1)}, bf16[128,4096]{1,0:T(8,128)(2,1)}, u32[]{:S(2)}, u32[]{:S(2)}) collective-permute-start(bf16[128,4096]{1,0:T(8,128)(2,1)S(1)} %get-tuple-element.43.refs_0_), channel_id=1, source_target_pairs={{0,7},{1,0},{2,1},{3,2},{4,3},{5,4},{6,5},{7,6},{8,15},{9,8},{10,9... | collective-permute-start | bytes 3145736 | tf_op jit(solution)/shard_map/ppermute | solution.py:37
  8.9 27.0 %collective-permute-start = (bf16[128,4096]{1,0:T(8,128)(2,1)S(1)}, bf16[128,4096]{1,0:T(8,128)(2,1)}, u32[]{:S(2)}, u32[]{:S(2)}) collective-permute-start(bf16[128,4096]{1,0:T(8,128)(2,1)S(1)} %get-tuple-element.43.refs_0_), channel_id=1, source_target_pairs={{0,1},{1,2},{2,3},{3,4},{4,5},{5,6},{6,7},{7,0},{8,9},{9,10},{10,1... | collective-permute-start | bytes 3145736 | tf_op jit(solution)/shard_map/ppermute | solution.py:37
  9.9 25.9 %all-to-all-start = ((f32[8,32,128]{2,1,0:T(8,128)}), f32[8,32,128]{2,1,0:T(8,128)S(1)}, u32[]{:S(2)}, u32[]{:S(2)}) async-start(f32[8,32,128]{2,1,0:T(8,128)} %bitcast_bitcast_fusion.1), calls=%async_computation | async-start | bytes 262144 | tf_op jit(solution)/shard_map/all_to_all | solution.py:242
  14.0 55.5 %collective-permute-start.3 = (bf16[128,4096]{1,0:T(8,128)(2,1)S(1)}, bf16[128,4096]{1,0:T(8,128)(2,1)}, u32[]{:S(2)}, u32[]{:S(2)}) collective-permute-start(bf16[128,4096]{1,0:T(8,128)(2,1)S(1)} %get-tuple-element.23.refs_0_), channel_id=1, source_target_pairs={{0,7},{1,0},{2,1},{3,2},{4,3},{5,4},{6,5},{7,6},{8,15},{9,8},{10,9... | collective-permute-start | bytes 3145736 | tf_op jit(solution)/shard_map/ppermute | solution.py:37
  16.7 52.9 %collective-permute-start.2 = (bf16[128,4096]{1,0:T(8,128)(2,1)S(1)}, bf16[128,4096]{1,0:T(8,128)(2,1)}, u32[]{:S(2)}, u32[]{:S(2)}) collective-permute-start(bf16[128,4096]{1,0:T(8,128)(2,1)S(1)} %get-tuple-element.23.refs_0_), channel_id=1, source_target_pairs={{0,1},{1,2},{2,3},{3,4},{4,5},{5,6},{6,7},{7,0},{8,9},{9,10},{10,1... | collective-permute-start | bytes 3145736 | tf_op jit(solution)/shard_map/ppermute | solution.py:37
  35.9 2.8 %copy-start = (bf16[1,8192,256]{2,1,0:T(8,128)(2,1)S(1)}, bf16[1,8192,256]{2,1,0:T(8,128)(2,1)}, u32[]{:S(2)}) copy-start(bf16[1,8192,256]{2,1,0:T(8,128)(2,1)} %param.6) | copy-start | bytes 12582916
  41.4 28.1 %all-to-all-start.1 = ((f32[32,32,256]{2,1,0:T(8,128)}), f32[32,32,256]{2,1,0:T(8,128)S(1)}, u32[]{:S(2)}, u32[]{:S(2)}) async-start(f32[32,32,256]{2,1,0:T(8,128)} %bitcast.45), calls=%async_computation.1 | async-start | bytes 2097152 | tf_op jit(solution)/shard_map/all_to_all | solution.py:247
  52.6 33.4 %collective-permute-start.5 = (bf16[128,4096]{1,0:T(8,128)(2,1)}, bf16[128,4096]{1,0:T(8,128)(2,1)}, u32[]{:S(2)}, u32[]{:S(2)}) collective-permute-start(bf16[128,4096]{1,0:T(8,128)(2,1)} %collective-permute-done.1.refs_1_), channel_id=1, source_target_pairs={{0,7},{1,0},{2,1},{3,2},{4,3},{5,4},{6,5},{7,6},{8,15},{9,8},{10,9... | collective-permute-start | bytes 3145736 | tf_op jit(solution)/shard_map/ppermute | solution.py:37
  52.7 33.3 %collective-permute-start.4 = (bf16[128,4096]{1,0:T(8,128)(2,1)}, bf16[128,4096]{1,0:T(8,128)(2,1)}, u32[]{:S(2)}, u32[]{:S(2)}) collective-permute-start(bf16[128,4096]{1,0:T(8,128)(2,1)} %collective-permute-done.refs_6_), channel_id=1, source_target_pairs={{0,1},{1,2},{2,3},{3,4},{4,5},{5,6},{6,7},{7,0},{8,9},{9,10},{10,1... | collective-permute-start | bytes 3145736 | tf_op jit(solution)/shard_map/ppermute | solution.py:37
  70.3 15.6 %all-to-all-start.2 = ((f32[8,32,256]{2,1,0:T(8,128)}), f32[8,32,256]{2,1,0:T(8,128)S(1)}, u32[]{:S(2)}, u32[]{:S(2)}) async-start(f32[8,32,256]{2,1,0:T(8,128)} %broadcast_in_dim.15), calls=%async_computation.2 | async-start | bytes 524288 | tf_op jit(solution)/shard_map/all_to_all | solution.py:250
  73.7 42.2 %collective-permute-start.6 = (bf16[128,4096]{1,0:T(8,128)(2,1)}, bf16[128,4096]{1,0:T(8,128)(2,1)}, u32[]{:S(2)}, u32[]{:S(2)}) collective-permute-start(bf16[128,4096]{1,0:T(8,128)(2,1)} %collective-permute-done.2.refs_6_), channel_id=1, source_target_pairs={{0,1},{1,2},{2,3},{3,4},{4,5},{5,6},{6,7},{7,0},{8,9},{9,10},{10,1... | collective-permute-start | bytes 3145736 | tf_op jit(solution)/shard_map/ppermute | solution.py:37
  75.1 40.9 %collective-permute-start.7 = (bf16[128,4096]{1,0:T(8,128)(2,1)}, bf16[128,4096]{1,0:T(8,128)(2,1)}, u32[]{:S(2)}, u32[]{:S(2)}) collective-permute-start(bf16[128,4096]{1,0:T(8,128)(2,1)} %collective-permute-done.3.refs_1_), channel_id=1, source_target_pairs={{0,7},{1,0},{2,1},{3,2},{4,3},{5,4},{6,5},{7,6},{8,15},{9,8},{10,9... | collective-permute-start | bytes 3145736 | tf_op jit(solution)/shard_map/ppermute | solution.py:37
  87.1 28.8 %all-to-all-start.3 = ((f32[32,32,256]{2,1,0:T(8,128)}), f32[32,32,256]{2,1,0:T(8,128)S(1)}, u32[]{:S(2)}, u32[]{:S(2)}) async-start(f32[32,32,256]{2,1,0:T(8,128)} %broadcast_in_dim.16), calls=%async_computation.3 | async-start | bytes 2097152 | tf_op jit(solution)/shard_map/all_to_all | solution.py:257
  100.4 33.8 %collective-permute-start.8 = (bf16[128,4096]{1,0:T(8,128)(2,1)}, bf16[128,4096]{1,0:T(8,128)(2,1)}, u32[]{:S(2)}, u32[]{:S(2)}) collective-permute-start(bf16[128,4096]{1,0:T(8,128)(2,1)} %collective-permute-done.4.refs_5_), channel_id=1, source_target_pairs={{0,1},{1,2},{2,3},{3,4},{4,5},{5,6},{6,7},{7,0},{8,9},{9,10},{10,1... | collective-permute-start | bytes 3145736 | tf_op jit(solution)/shard_map/ppermute | solution.py:37
  100.5 33.7 %collective-permute-start.9 = (bf16[128,4096]{1,0:T(8,128)(2,1)}, bf16[128,4096]{1,0:T(8,128)(2,1)}, u32[]{:S(2)}, u32[]{:S(2)}) collective-permute-start(bf16[128,4096]{1,0:T(8,128)(2,1)} %collective-permute-done.5.refs_2_), channel_id=1, source_target_pairs={{0,7},{1,0},{2,1},{3,2},{4,3},{5,4},{6,5},{7,6},{8,15},{9,8},{10,9... | collective-permute-start | bytes 3145736 | tf_op jit(solution)/shard_map/ppermute | solution.py:37
  115.8 2.0 %copy-start.5 = (bf16[1,128,8192]{2,1,0:T(8,128)(2,1)S(1)}, bf16[1,128,8192]{2,1,0:T(8,128)(2,1)}, u32[]{:S(2)}) copy-start(bf16[1,128,8192]{2,1,0:T(8,128)(2,1)} %param.4) | copy-start | bytes 6291460
  115.9 1.0 copy-start.6
  117.1 1.5 copy-start.7
  117.1 1.5 copy-start.8
  117.1 1.5 copy-start.9
  119.3 14.9 %all-to-all-start.4 = ((f32[8,32,128]{2,1,0:T(8,128)}), f32[8,32,128]{2,1,0:T(8,128)S(1)}, u32[]{:S(2)}, u32[]{:S(2)}) async-start(f32[8,32,128]{2,1,0:T(8,128)} %broadcast_in_dim.17), calls=%async_computation.4 | async-start | bytes 262144 | tf_op jit(solution)/shard_map/all_to_all | solution.py:265
  124.1 42.1 %collective-permute-start.10 = (bf16[128,4096]{1,0:T(8,128)(2,1)}, bf16[128,4096]{1,0:T(8,128)(2,1)}, u32[]{:S(2)}, u32[]{:S(2)}) collective-permute-start(bf16[128,4096]{1,0:T(8,128)(2,1)} %collective-permute-done.6.refs_5_), channel_id=1, source_target_pairs={{0,1},{1,2},{2,3},{3,4},{4,5},{5,6},{6,7},{7,0},{8,9},{9,10},{10,1... | collective-permute-start | bytes 3145736 | tf_op jit(solution)/shard_map/ppermute | solution.py:37
  125.6 28.9 %collective-permute-start.11 = (bf16[128,4096]{1,0:T(8,128)(2,1)}, bf16[128,4096]{1,0:T(8,128)(2,1)}, u32[]{:S(2)}, u32[]{:S(2)}) collective-permute-start(bf16[128,4096]{1,0:T(8,128)(2,1)} %collective-permute-done.7.refs_2_), channel_id=1, source_target_pairs={{0,7},{1,0},{2,1},{3,2},{4,3},{5,4},{6,5},{7,6},{8,15},{9,8},{10,9... | collective-permute-start | bytes 3145736 | tf_op jit(solution)/shard_map/ppermute | solution.py:37
  140.1 28.2 %all-to-all-start.5 = ((f32[32,32,256]{2,1,0:T(8,128)}), f32[32,32,256]{2,1,0:T(8,128)}, u32[]{:S(2)}, u32[]{:S(2)}) async-start(f32[32,32,256]{2,1,0:T(8,128)} %broadcast_in_dim.18), calls=%async_computation.5 | async-start | bytes 2097152 | tf_op jit(solution)/shard_map/all_to_all | solution.py:272
  151.4 28.6 %collective-permute-start.12 = (bf16[128,4096]{1,0:T(8,128)(2,1)}, bf16[128,4096]{1,0:T(8,128)(2,1)}, u32[]{:S(2)}, u32[]{:S(2)}) collective-permute-start(bf16[128,4096]{1,0:T(8,128)(2,1)} %collective-permute-done.8.refs_4_), channel_id=1, source_target_pairs={{0,1},{1,2},{2,3},{3,4},{4,5},{5,6},{6,7},{7,0},{8,9},{9,10},{10,1... | collective-permute-start | bytes 3145736 | tf_op jit(solution)/shard_map/ppermute | solution.py:37
  154.4 25.6 %collective-permute-start.13 = (bf16[128,4096]{1,0:T(8,128)(2,1)}, bf16[128,4096]{1,0:T(8,128)(2,1)}, u32[]{:S(2)}, u32[]{:S(2)}) collective-permute-start(bf16[128,4096]{1,0:T(8,128)(2,1)} %collective-permute-done.11.refs_3_), channel_id=1, source_target_pairs={{0,7},{1,0},{2,1},{3,2},{4,3},{5,4},{6,5},{7,6},{8,15},{9,8},{10,9... | collective-permute-start | bytes 3145736 | tf_op jit(solution)/shard_map/ppermute | solution.py:37
  157.9 1.2 copy-start.4
  171.0 2.2 %copy-start.1 = (bf16[1,8192,256]{2,1,0:T(8,128)(2,1)S(1)}, bf16[1,8192,256]{2,1,0:T(8,128)(2,1)}, u32[]{:S(2)}) copy-start(bf16[1,8192,256]{2,1,0:T(8,128)(2,1)} %param.6) | copy-start | bytes 12582916
  173.2 6.9 %copy-start.2 = (f32[4096,256]{1,0:T(8,128)S(1)}, f32[4096,256]{1,0:T(8,128)}, u32[]{:S(2)}) copy-start(f32[4096,256]{1,0:T(8,128)} %shard_map.60.refs_2_) | copy-start | bytes 12582916

commit v4 on v3

--- a/solution.py
+++ b/solution.py
@@ -60,6 +60,13 @@
         self.down[c] = second = shift(after(self.down[c], *gate), self.axis, -1)
         self.blocks[c][hop] = second
         return first, second
+
+    def last(self, *gate):
+        pieces = []
+        for up, down in zip(self.up, self.down):
+            pieces.append(shift(after(up[:, :LAST], *gate), self.axis, 1))
+            pieces.append(shift(after(down[:, LAST:], *gate), self.axis, -1))
+        return pieces
 
 
 def factor_kernel(left_ref, inverse_ref):
@@ -178,8 +185,10 @@
     )(*blocks, cot, error)
 
 
-def finish_kernel(steps, first_ref, second_ref, one_ref, two_ref, left_ref, right_ref, cot_ref, out_ref):
+def finish_kernel(steps, a_ref, b_ref, c_ref, d_ref, one_ref, two_ref, left_ref, right_ref, cot_ref, out_ref):
     step = pl.program_id(0)
+    first = jnp.where(step == 0, a_ref[...], b_ref[...])
+    second = jnp.where(step == steps, c_ref[...], d_ref[...])
 
     @pl.when(step < steps)
     def _():
@@ -187,15 +196,15 @@
         high, middle, low = (left_ref[k * rank : (k + 1) * rank, :] for k in range(3))
         left = jnp.concatenate([high, middle, high, middle, low, high], axis=0)
         product = dot(left, right_ref[...], ((0,), (0,)))
-        out_ref[...] = (one_ref[...] + dot(first_ref[...], cot_ref[...], ((0,), (0,))) + product).astype(BF16)
+        out_ref[...] = (one_ref[...] + dot(first, cot_ref[...], ((0,), (0,))) + product).astype(BF16)
 
     @pl.when(step >= steps)
     def _():
-        out_ref[...] = (two_ref[...] + dot(second_ref[...], cot_ref[...], ((0,), (0,)))).astype(BF16)
-
-
-def finish(first, second, one, two, left3, right_wide, cot):
-    depth, width = first.shape
+        out_ref[...] = (two_ref[...] + dot(second, cot_ref[...], ((0,), (0,)))).astype(BF16)
+
+
+def finish(far, one, two, left3, right_wide, cot):
+    depth, width = far[0].shape[0], one.shape[0]
     columns = cot.shape[1]
     steps = width // LAST
     low = lambda i: jnp.minimum(i, steps - 1)
@@ -204,8 +213,7 @@
         lambda *refs: finish_kernel(steps, *refs),
         grid=(2 * steps,),
         in_specs=[
-            pl.BlockSpec((depth, LAST), lambda i: (0, low(i))),
-            pl.BlockSpec((depth, LAST), lambda i: (0, high(i))),
+            *[pl.BlockSpec((depth, LAST), lambda i: (0, 0)) for _ in far],
             pl.BlockSpec((LAST, columns), lambda i: (low(i), 0)),
             pl.BlockSpec((LAST, columns), lambda i: (high(i), 0)),
             pl.BlockSpec((left3.shape[0], LAST), lambda i: (0, low(i))),
@@ -218,7 +226,7 @@
         cost_estimate=pl.CostEstimate(
             flops=4 * depth * width * columns, bytes_accessed=4 * width * (depth + 3 * columns), transcendentals=0
         ),
-    )(first, second, one, two, left3, right_wide, cot)
+    )(*far, one, two, left3, right_wide, cot)
 
 
 def spread(x, axis):
@@ -266,14 +274,14 @@
     inner = after(inner, inverse, mine, *moved[4])
     right_part = join_rows(dot(split_rows(inner), cot, ((1,), (0,))) + dot(left3, error, ((1,), (0,))))
     right_part = spread(right_part, "dp")
-    moved.append(ring.step(right_part))
+    far = ring.last(right_part)
     blocks = ring.blocks
     one = early_partial(0, blocks[0][:half] + blocks[0][half + 1 :], early, error)
     parts = after(lax.all_to_all(right_part, "dp", 0, 0), one, *moved[5])
     decompressed, right_wide = solve(inverse, parts, mine)
 
     two = partial(width, blocks[1][:half] + blocks[1][half + 1 :], early, right_wide, left3, error)
-    out = finish(blocks[0][half], blocks[1][half], one, two, left3, right_wide, cot_last)
+    out = finish(far, one, two, left3, right_wide, cot_last)
     return decompressed, out[None]
 
 

time: 187 us -> 190 us (1.016)
  local copies, waits for them, and re-layouts: 12.8 us -> 21.2 us
  waiting for transfers between devices: 64.5 us -> 56.1 us
    slice x0 -> x4, local copies, waits for them, and re-layouts: none -> 7.63 us  [the longest x2 3.83 us: last(): pieces.append(shift(after(up[:, :LAST], *gate), self.axis, 1))]
    ppermute x14 -> x16, waiting for transfers between devices: 3.29 us -> 0.04 us  [shift(): return lax.ppermute(x, axis, [(j, (j + by) % size) for j in range(size)])]
    all_to_all x1, waiting for transfers between devices: 2.14 us -> 0.01 us  [shards(): parts = after(lax.all_to_all(right_part, 'dp', 0, 0), one, *moved[5])]
    unnamed x24 -> x28, local copies, waits for them, and re-layouts: 5.47 us -> 3.98 us
    ppermute x14 -> x16, starting transfers between devices: 23.2 us -> 24.3 us  [shift(): return lax.ppermute(x, axis, [(j, (j + by) % size) for j in range(size)])]
  transfers between devices with their start and end apart: 20 -> 22, of which waited for: 8 -> 5; matrix products, arithmetic and copies ran while one was open for 10% -> 16% of each run, Pallas kernels for 11% -> 11%
where the time goes in v4:
time: 190 us; the launch traced here: 188 us
  starting transfers between devices  69.6 us (37%)
  waiting for transfers between devices  56.1 us (30%)
  Pallas kernels  25.7 us (14%)
  local copies, waits for them, and re-layouts  21.2 us (11%)
  matrix products  9.53 us (5%)
  other arithmetic  5.03 us (3%)
    ppermute x16, starting transfers between devices, shift(): return lax.ppermute(x, axis, [(j, (j + by) % size) for j in range(size)])  24.3 us
    all_to_all x1, waiting for transfers between devices, shards(): lax.all_to_all(weights, 'tensor', 0, 0)  19.2 us
    all_to_all x1, waiting for transfers between devices, shards(): lax.all_to_all(left_part, 'dp', 0, 0)  15.4 us
    all_to_all x1, starting transfers between devices, shards(): left = lax.all_to_all(spread(whole_rows, 'dp'), 'dp', 0, 0)  12 us
    all_to_all x1, starting transfers between devices, shards(): parts = after(lax.all_to_all(right_part, 'dp', 0, 0), one, *moved[5])  11.2 us
    all_to_all x1, starting transfers between devices, shards(): lax.all_to_all(left_part, 'dp', 0, 0)  11.2 us
    all_to_all x1, waiting for transfers between devices, shards(): left = lax.all_to_all(spread(whole_rows, 'dp'), 'dp', 0, 0)  11 us
    dot_general x6, matrix products, dot(): return lax.dot_general(a, b, (dims, ((), ())), preferred_element_type=F32)  9.53 us
  transfers between devices with their start and end apart: 22, of which 5 were waited for; matrix products, arithmetic and copies ran while one was open for 16% of the time, Pallas kernels for 11%

profile of v4, /device:TPU:1, one launch (start us, length us, event | category | flops | bytes accessed | tf_op | source)
XLA Modules:
  0.0 188.1 jit_solution(11048073862856258172)
XLA Ops:
  0.7 1.8 fusion.30
  2.5 6.5 %collective-permute-start.1 = (bf16[128,4096]{1,0:T(8,128)(2,1)S(1)}, bf16[128,4096]{1,0:T(8,128)(2,1)}, u32[]{:S(2)}, u32[]{:S(2)}) collective-permute-start(bf16[128,4096]{1,0:T(8,128)(2,1)S(1)} %get-tuple-element.47.refs_0_), channel_id=1, source_target_pairs={{0,7},{1,0},{2,1},{3,2},{4,3},{5,4},{6,5},{7,6},{8,15},{9,8},{10,9... | collective-permute-start | bytes 3145736 | tf_op jit(solution)/shard_map/ppermute | solution.py:37
  10.0 4.1 %all-to-all-start = ((f32[8,32,128]{2,1,0:T(8,128)}), f32[8,32,128]{2,1,0:T(8,128)S(1)}, u32[]{:S(2)}, u32[]{:S(2)}) async-start(f32[8,32,128]{2,1,0:T(8,128)} %bitcast_bitcast_fusion.1), calls=%async_computation | async-start | bytes 262144 | tf_op jit(solution)/shard_map/all_to_all | solution.py:250
  14.0 2.7 %collective-permute-start.3 = (bf16[128,4096]{1,0:T(8,128)(2,1)S(1)}, bf16[128,4096]{1,0:T(8,128)(2,1)}, u32[]{:S(2)}, u32[]{:S(2)}) collective-permute-start(bf16[128,4096]{1,0:T(8,128)(2,1)S(1)} %get-tuple-element.25.refs_0_), channel_id=1, source_target_pairs={{0,7},{1,0},{2,1},{3,2},{4,3},{5,4},{6,5},{7,6},{8,15},{9,8},{10,9... | collective-permute-start | bytes 3145736 | tf_op jit(solution)/shard_map/ppermute | solution.py:37
  16.7 19.2 %all-to-all-done = f32[8,32,128]{2,1,0:T(8,128)S(1)} async-done(((f32[8,32,128]{2,1,0:T(8,128)}), f32[8,32,128]{2,1,0:T(8,128)S(1)}, u32[]{:S(2)}, u32[]{:S(2)}) %all-to-all-start) | async-done | bytes 131104 | tf_op jit(solution)/shard_map/all_to_all | solution.py:250
  36.0 2.3 %fusion.11 = f32[96,8192]{1,0:T(8,128)S(1)} fusion(bf16[32,128]{1,0:T(8,128)(2,1)S(1)} %get-tuple-element.58, bf16[32,128]{1,0:T(8,128)(2,1)S(1)} %get-tuple-element.59, bf16[32,128]{1,0:T(8,128)(2,1)S(1)} %get-tuple-element.57, bf16[1,128,8192]{2,1,0:T(8,128)(2,1)} %param.4), kind=kOutput, calls=%fused_computation.39 | convolution fusion | flops 201400320 | bytes 5267456 | tf_op jit(solution)/shard_map/dot_general | solution.py:32
  38.7 1.4 convolution_add_fusion
  40.3 1.1 copy.21
  41.4 11.2 %all-to-all-start.1 = ((f32[32,32,256]{2,1,0:T(8,128)}), f32[32,32,256]{2,1,0:T(8,128)S(1)}, u32[]{:S(2)}, u32[]{:S(2)}) async-start(f32[32,32,256]{2,1,0:T(8,128)} %bitcast.45), calls=%async_computation.1 | async-start | bytes 2097152 | tf_op jit(solution)/shard_map/all_to_all | solution.py:255
  52.7 1.5 collective-permute-start.4
  54.2 15.4 %all-to-all-done.1 = f32[32,32,256]{2,1,0:T(8,128)S(1)} async-done(((f32[32,32,256]{2,1,0:T(8,128)}), f32[32,32,256]{2,1,0:T(8,128)S(1)}, u32[]{:S(2)}, u32[]{:S(2)}) %all-to-all-start.1) | async-done | bytes 1048608 | tf_op jit(solution)/shard_map/all_to_all | solution.py:255
  69.6 0.7 broadcast_in_dim.15
  70.3 3.4 %all-to-all-start.2 = ((f32[8,32,256]{2,1,0:T(8,128)}), f32[8,32,256]{2,1,0:T(8,128)S(1)}, u32[]{:S(2)}, u32[]{:S(2)}) async-start(f32[8,32,256]{2,1,0:T(8,128)} %broadcast_in_dim.15), calls=%async_computation.2 | async-start | bytes 524288 | tf_op jit(solution)/shard_map/all_to_all | solution.py:258
  73.8 1.4 collective-permute-start.6
  75.1 1.4 collective-permute-start.7
  76.5 9.3 %all-to-all-done.2 = f32[8,32,256]{2,1,0:T(8,128)S(1)} async-done(((f32[8,32,256]{2,1,0:T(8,128)}), f32[8,32,256]{2,1,0:T(8,128)S(1)}, u32[]{:S(2)}, u32[]{:S(2)}) %all-to-all-start.2) | async-done | bytes 262176 | tf_op jit(solution)/shard_map/all_to_all | solution.py:258
  85.9 1.2 broadcast_in_dim.16
  87.2 12.0 %all-to-all-start.3 = ((f32[32,32,256]{2,1,0:T(8,128)}), f32[32,32,256]{2,1,0:T(8,128)S(1)}, u32[]{:S(2)}, u32[]{:S(2)}) async-start(f32[32,32,256]{2,1,0:T(8,128)} %broadcast_in_dim.16), calls=%async_computation.3 | async-start | bytes 2097152 | tf_op jit(solution)/shard_map/all_to_all | solution.py:265
  99.2 1.4 fusion.1
  100.6 0.7 slice.93
  101.3 1.0 pad_maximum_fusion.1.refs_7_
  102.4 2.7 %collective-permute-start.9 = (bf16[128,4096]{1,0:T(8,128)(2,1)}, bf16[128,4096]{1,0:T(8,128)(2,1)}, u32[]{:S(2)}, u32[]{:S(2)}) collective-permute-start(bf16[128,4096]{1,0:T(8,128)(2,1)} %collective-permute-done.5.refs_2_), channel_id=1, source_target_pairs={{0,7},{1,0},{2,1},{3,2},{4,3},{5,4},{6,5},{7,6},{8,15},{9,8},{10,9... | collective-permute-start | bytes 3145736 | tf_op jit(solution)/shard_map/ppermute | solution.py:37
  105.0 11.0 %all-to-all-done.3 = f32[32,32,256]{2,1,0:T(8,128)S(1)} async-done(((f32[32,32,256]{2,1,0:T(8,128)}), f32[32,32,256]{2,1,0:T(8,128)S(1)}, u32[]{:S(2)}, u32[]{:S(2)}) %all-to-all-start.3) | async-done | bytes 1048608 | tf_op jit(solution)/shard_map/all_to_all | solution.py:265
  116.1 1.0 copy-done.7
  117.1 1.5 copy.16
  119.0 0.8 fusion.25
  120.5 3.4 %all-to-all-start.4 = ((f32[8,32,128]{2,1,0:T(8,128)}), f32[8,32,128]{2,1,0:T(8,128)S(1)}, u32[]{:S(2)}, u32[]{:S(2)}) async-start(f32[8,32,128]{2,1,0:T(8,128)} %broadcast_in_dim.17), calls=%async_computation.4 | async-start | bytes 262144 | tf_op jit(solution)/shard_map/all_to_all | solution.py:273
  123.9 1.5 pad_maximum_fusion.left_ref.refs_9_.refs_6_
  125.4 1.4 collective-permute-start.10
  126.8 1.3 collective-permute-start.11
  128.1 4.2 %shard_map.59.inverse_ref = f32[32,32]{1,0:T(8,128)S(1)} custom-call(bf16[96,8192]{1,0:T(8,128)(2,1)S(1)} %pad_maximum_fusion.left_ref.refs_9_.refs_6_), custom_call_target="tpu_custom_call" | custom-call | flops 16777216 | bytes 3145728 | tf_op jit(solution)/shard_map/pallas_call | solution.py:92
  132.4 0.8 constant_dynamic-slice_fusion.mine_ref
  133.1 1.1 all-to-all-done.4
  134.3 1.3 fusion.2
  135.6 3.5 %convolution_add_fusion.1 = f32[96,256]{1,0:T(8,128)S(1)} fusion(f32[96,256]{1,0:T(8,128)S(1)} %fusion.2, bf16[1,8192,256]{2,1,0:T(8,128)(2,1)} %param.6, bf16[32,8192]{1,0:T(8,128)(2,1)} %copy-done.9, bf16[32,8192]{1,0:T(8,128)(2,1)} %copy-done.10, bf16[32,8192]{1,0:T(8,128)(2,1)} %copy-done.8), kind=kOutput, calls=%fused_computation.6 | convolution fusion | flops 407396352 | bytes 5963776 | tf_op jit(solution)/shard_map/dot_general | solution.py:32
  139.1 1.1 broadcast_in_dim.18
  140.2 11.2 %all-to-all-start.5 = ((f32[32,32,256]{2,1,0:T(8,128)}), f32[32,32,256]{2,1,0:T(8,128)}, u32[]{:S(2)}, u32[]{:S(2)}) async-start(f32[32,32,256]{2,1,0:T(8,128)} %broadcast_in_dim.18), calls=%async_computation.5 | async-start | bytes 2097152 | tf_op jit(solution)/shard_map/all_to_all | solution.py:280
  151.4 2.0 %slice.101 = bf16[128,2048]{1,0:T(8,128)(2,1)} slice(bf16[128,4096]{1,0:T(8,128)(2,1)} %collective-permute-done.8.refs_4_), slice={[0:128], [0:2048]} | slice | bytes 1048576 | tf_op jit(solution)/shard_map/slice | solution.py:67
  153.4 1.9 %slice.102 = bf16[128,2048]{1,0:T(8,128)(2,1)} slice(bf16[128,4096]{1,0:T(8,128)(2,1)} %collective-permute-done.9.refs_3_), slice={[0:128], [2048:4096]} | slice | bytes 1048576 | tf_op jit(solution)/shard_map/slice | solution.py:68
  156.0 2.0 %collective-permute-start.13 = (bf16[128,2048]{1,0:T(8,128)(2,1)}, bf16[128,2048]{1,0:T(8,128)(2,1)}, u32[]{:S(2)}, u32[]{:S(2)}) collective-permute-start(bf16[128,2048]{1,0:T(8,128)(2,1)} %slice.102), channel_id=1, source_target_pairs={{0,7},{1,0},{2,1},{3,2},{4,3},{5,4},{6,5},{7,6},{8,15},{9,8},{10,9... | collective-permute-start | bytes 1572872 | tf_op jit(solution)/shard_map/ppermute | solution.py:37
  158.0 1.9 %slice.104 = bf16[128,2048]{1,0:T(8,128)(2,1)} slice(bf16[128,4096]{1,0:T(8,128)(2,1)} %collective-permute-done.11.refs_3_), slice={[0:128], [2048:4096]} | slice | bytes 1048576 | tf_op jit(solution)/shard_map/slice | solution.py:68
  159.9 1.9 slice.103
  161.7 2.7 %collective-permute-start.15 = (bf16[128,2048]{1,0:T(8,128)(2,1)}, bf16[128,2048]{1,0:T(8,128)(2,1)}, u32[]{:S(2)}, u32[]{:S(2)}) collective-permute-start(bf16[128,2048]{1,0:T(8,128)(2,1)} %slice.104), channel_id=1, source_target_pairs={{0,7},{1,0},{2,1},{3,2},{4,3},{5,4},{6,5},{7,6},{8,15},{9,8},{10,9... | collective-permute-start | bytes 1572872 | tf_op jit(solution)/shard_map/ppermute | solution.py:37
  164.4 7.1 %shard_map.60.refs_4_ = f32[4096,256]{1,0:T(8,128)} custom-call(bf16[128,4096]{1,0:T(8,128)(2,1)S(1)} %copy-done.4, bf16[128,4096]{1,0:T(8,128)(2,1)} %collective-permute-done.1.refs_1_, bf16[128,4096]{1,0:T(8,128)(2,1)} %collective-permute-done.5.refs_2_, bf16[128,4096]{1,0:T(8,128)(2,1)} %collective-permute-done.9.refs_3_, ...), custom_call_target="tpu_custom_call" | custom-call | flops 1048576 | bytes 65536 | tf_op jit(solution)/shard_map/pallas_call | solution.py:173
  171.6 2.6 %shard_map.61 = (bf16[256,256]{1,0:T(8,128)(2,1)}, bf16[192,256]{1,0:T(8,128)(2,1)S(1)}) custom-call(f32[32,32]{1,0:T(8,128)S(1)} %shard_map.59.inverse_ref, f32[32,32,256]{2,1,0:T(8,128)} %all-to-all-done.5.parts_ref, f32[32,256]{1,0:T(8,128)S(1)} %constant_dynamic-slice_fusion.mine_ref), custom_call_target="tpu_custom_call" | custom-call | flops 16777216 | bytes 1048576 | tf_op jit(solution)/shard_map/pallas_call | solution.py:117
  174.2 2.2 %copy-done.1 = bf16[1,8192,256]{2,1,0:T(8,128)(2,1)S(1)} copy-done((bf16[1,8192,256]{2,1,0:T(8,128)(2,1)S(1)}, bf16[1,8192,256]{2,1,0:T(8,128)(2,1)}, u32[]{:S(2)}) %copy-start.1) | copy-done | bytes 4194328
  176.4 5.9 %shard_map.62.refs_5_ = f32[4096,256]{1,0:T(8,128)S(1)} custom-call(bf16[128,4096]{1,0:T(8,128)(2,1)S(1)} %get-tuple-element.25.refs_0_, bf16[128,4096]{1,0:T(8,128)(2,1)} %collective-permute-done.3.refs_1_, bf16[128,4096]{1,0:T(8,128)(2,1)} %collective-permute-done.7.refs_2_, bf16[128,4096]{1,0:T(8,128)(2,1)} %collective-permute-done.11.refs_3_, ...), custom_call_target="tpu_custom_call" | custom-call | flops 1879048192 | bytes 13631488 | tf_op jit(solution)/shard_map/pallas_call | solution.py:144
  182.3 5.8 %shard_map.63 = bf16[8192,256]{1,0:T(8,128)(2,1)} custom-call(bf16[128,2048]{1,0:T(8,128)(2,1)} %collective-permute-done.12.refs_0_, bf16[128,2048]{1,0:T(8,128)(2,1)} %collective-permute-done.13.refs_1_, bf16[128,2048]{1,0:T(8,128)(2,1)} %collective-permute-done.14.refs_2_, bf16[128,2048]{1,0:T(8,128)(2,1)} %collective-permute-done.15.refs_3_, ...), custom_call_target="tpu_custom_call" | custom-call | flops 536870912 | bytes 14680064 | tf_op jit(solution)/shard_map/pallas_call | solution.py:212
  (65 shorter events, 3.9 us)
Async XLA Ops:
  0.6 8.3 %copy-start.13 = (f32[256,32]{0,1:T(8,128)S(1)}, f32[256,32]{0,1:T(8,128)}, u32[]{:S(2)}) copy-start(f32[256,32]{0,1:T(8,128)} %param.7) | copy-start | bytes 98308
  0.6 8.3 %copy-start.11 = (bf16[1,1024,256]{2,1,0:T(8,128)(2,1)S(1)}, bf16[1,1024,256]{2,1,0:T(8,128)(2,1)}, u32[]{:S(2)}) copy-start(bf16[1,1024,256]{2,1,0:T(8,128)(2,1)} %param.5) | copy-start | bytes 1572868
  2.5 35.8 %copy-start.3 = (bf16[128,4096]{1,0:T(8,128)(2,1)}, bf16[128,4096]{1,0:T(8,128)(2,1)S(1)}, u32[]{:S(2)}) copy-start(bf16[128,4096]{1,0:T(8,128)(2,1)S(1)} %get-tuple-element.47.refs_0_) | copy-start | bytes 3145732
  2.5 33.5 %collective-permute-start.1 = (bf16[128,4096]{1,0:T(8,128)(2,1)S(1)}, bf16[128,4096]{1,0:T(8,128)(2,1)}, u32[]{:S(2)}, u32[]{:S(2)}) collective-permute-start(bf16[128,4096]{1,0:T(8,128)(2,1)S(1)} %get-tuple-element.47.refs_0_), channel_id=1, source_target_pairs={{0,7},{1,0},{2,1},{3,2},{4,3},{5,4},{6,5},{7,6},{8,15},{9,8},{10,9... | collective-permute-start | bytes 3145736 | tf_op jit(solution)/shard_map/ppermute | solution.py:37
  9.0 27.0 %collective-permute-start = (bf16[128,4096]{1,0:T(8,128)(2,1)S(1)}, bf16[128,4096]{1,0:T(8,128)(2,1)}, u32[]{:S(2)}, u32[]{:S(2)}) collective-permute-start(bf16[128,4096]{1,0:T(8,128)(2,1)S(1)} %get-tuple-element.47.refs_0_), channel_id=1, source_target_pairs={{0,1},{1,2},{2,3},{3,4},{4,5},{5,6},{6,7},{7,0},{8,9},{9,10},{10,1... | collective-permute-start | bytes 3145736 | tf_op jit(solution)/shard_map/ppermute | solution.py:37
  10.0 25.9 %all-to-all-start = ((f32[8,32,128]{2,1,0:T(8,128)}), f32[8,32,128]{2,1,0:T(8,128)S(1)}, u32[]{:S(2)}, u32[]{:S(2)}) async-start(f32[8,32,128]{2,1,0:T(8,128)} %bitcast_bitcast_fusion.1), calls=%async_computation | async-start | bytes 262144 | tf_op jit(solution)/shard_map/all_to_all | solution.py:250
  14.0 55.6 %collective-permute-start.3 = (bf16[128,4096]{1,0:T(8,128)(2,1)S(1)}, bf16[128,4096]{1,0:T(8,128)(2,1)}, u32[]{:S(2)}, u32[]{:S(2)}) collective-permute-start(bf16[128,4096]{1,0:T(8,128)(2,1)S(1)} %get-tuple-element.25.refs_0_), channel_id=1, source_target_pairs={{0,7},{1,0},{2,1},{3,2},{4,3},{5,4},{6,5},{7,6},{8,15},{9,8},{10,9... | collective-permute-start | bytes 3145736 | tf_op jit(solution)/shard_map/ppermute | solution.py:37
  16.7 52.9 %collective-permute-start.2 = (bf16[128,4096]{1,0:T(8,128)(2,1)S(1)}, bf16[128,4096]{1,0:T(8,128)(2,1)}, u32[]{:S(2)}, u32[]{:S(2)}) collective-permute-start(bf16[128,4096]{1,0:T(8,128)(2,1)S(1)} %get-tuple-element.25.refs_0_), channel_id=1, source_target_pairs={{0,1},{1,2},{2,3},{3,4},{4,5},{5,6},{6,7},{7,0},{8,9},{9,10},{10,1... | collective-permute-start | bytes 3145736 | tf_op jit(solution)/shard_map/ppermute | solution.py:37
  35.9 2.8 %copy-start = (bf16[1,8192,256]{2,1,0:T(8,128)(2,1)S(1)}, bf16[1,8192,256]{2,1,0:T(8,128)(2,1)}, u32[]{:S(2)}) copy-start(bf16[1,8192,256]{2,1,0:T(8,128)(2,1)} %param.6) | copy-start | bytes 12582916
  41.4 28.1 %all-to-all-start.1 = ((f32[32,32,256]{2,1,0:T(8,128)}), f32[32,32,256]{2,1,0:T(8,128)S(1)}, u32[]{:S(2)}, u32[]{:S(2)}) async-start(f32[32,32,256]{2,1,0:T(8,128)} %bitcast.45), calls=%async_computation.1 | async-start | bytes 2097152 | tf_op jit(solution)/shard_map/all_to_all | solution.py:255
  52.6 33.3 %collective-permute-start.5 = (bf16[128,4096]{1,0:T(8,128)(2,1)}, bf16[128,4096]{1,0:T(8,128)(2,1)}, u32[]{:S(2)}, u32[]{:S(2)}) collective-permute-start(bf16[128,4096]{1,0:T(8,128)(2,1)} %collective-permute-done.1.refs_1_), channel_id=1, source_target_pairs={{0,7},{1,0},{2,1},{3,2},{4,3},{5,4},{6,5},{7,6},{8,15},{9,8},{10,9... | collective-permute-start | bytes 3145736 | tf_op jit(solution)/shard_map/ppermute | solution.py:37
  52.7 33.2 %collective-permute-start.4 = (bf16[128,4096]{1,0:T(8,128)(2,1)}, bf16[128,4096]{1,0:T(8,128)(2,1)S(1)}, u32[]{:S(2)}, u32[]{:S(2)}) collective-permute-start(bf16[128,4096]{1,0:T(8,128)(2,1)} %collective-permute-done.refs_6_), channel_id=1, source_target_pairs={{0,1},{1,2},{2,3},{3,4},{4,5},{5,6},{6,7},{7,0},{8,9},{9,10},{10,1... | collective-permute-start | bytes 3145736 | tf_op jit(solution)/shard_map/ppermute | solution.py:37
  70.3 15.5 %all-to-all-start.2 = ((f32[8,32,256]{2,1,0:T(8,128)}), f32[8,32,256]{2,1,0:T(8,128)S(1)}, u32[]{:S(2)}, u32[]{:S(2)}) async-start(f32[8,32,256]{2,1,0:T(8,128)} %broadcast_in_dim.15), calls=%async_computation.2 | async-start | bytes 524288 | tf_op jit(solution)/shard_map/all_to_all | solution.py:258
  73.8 44.8 %collective-permute-start.6 = (bf16[128,4096]{1,0:T(8,128)(2,1)}, bf16[128,4096]{1,0:T(8,128)(2,1)}, u32[]{:S(2)}, u32[]{:S(2)}) collective-permute-start(bf16[128,4096]{1,0:T(8,128)(2,1)} %collective-permute-done.2.refs_6_), channel_id=1, source_target_pairs={{0,1},{1,2},{2,3},{3,4},{4,5},{5,6},{6,7},{7,0},{8,9},{9,10},{10,1... | collective-permute-start | bytes 3145736 | tf_op jit(solution)/shard_map/ppermute | solution.py:37
  75.1 43.4 %collective-permute-start.7 = (bf16[128,4096]{1,0:T(8,128)(2,1)}, bf16[128,4096]{1,0:T(8,128)(2,1)}, u32[]{:S(2)}, u32[]{:S(2)}) collective-permute-start(bf16[128,4096]{1,0:T(8,128)(2,1)} %collective-permute-done.3.refs_1_), channel_id=1, source_target_pairs={{0,7},{1,0},{2,1},{3,2},{4,3},{5,4},{6,5},{7,6},{8,15},{9,8},{10,9... | collective-permute-start | bytes 3145736 | tf_op jit(solution)/shard_map/ppermute | solution.py:37
  85.9 1.3 copy-start.12
  87.2 28.9 %all-to-all-start.3 = ((f32[32,32,256]{2,1,0:T(8,128)}), f32[32,32,256]{2,1,0:T(8,128)S(1)}, u32[]{:S(2)}, u32[]{:S(2)}) async-start(f32[32,32,256]{2,1,0:T(8,128)} %broadcast_in_dim.16), calls=%async_computation.3 | async-start | bytes 2097152 | tf_op jit(solution)/shard_map/all_to_all | solution.py:265
  102.3 32.0 %collective-permute-start.8 = (bf16[128,4096]{1,0:T(8,128)(2,1)}, bf16[128,4096]{1,0:T(8,128)(2,1)}, u32[]{:S(2)}, u32[]{:S(2)}) collective-permute-start(bf16[128,4096]{1,0:T(8,128)(2,1)} %copy-done.12), channel_id=1, source_target_pairs={{0,1},{1,2},{2,3},{3,4},{4,5},{5,6},{6,7},{7,0},{8,9},{9,10},{10,1... | collective-permute-start | bytes 3145736 | tf_op jit(solution)/shard_map/ppermute | solution.py:37
  102.4 31.9 %collective-permute-start.9 = (bf16[128,4096]{1,0:T(8,128)(2,1)}, bf16[128,4096]{1,0:T(8,128)(2,1)}, u32[]{:S(2)}, u32[]{:S(2)}) collective-permute-start(bf16[128,4096]{1,0:T(8,128)(2,1)} %collective-permute-done.5.refs_2_), channel_id=1, source_target_pairs={{0,7},{1,0},{2,1},{3,2},{4,3},{5,4},{6,5},{7,6},{8,15},{9,8},{10,9... | collective-permute-start | bytes 3145736 | tf_op jit(solution)/shard_map/ppermute | solution.py:37
  116.1 1.0 copy-start.7
  117.1 1.9 %copy-start.5 = (bf16[1,128,8192]{2,1,0:T(8,128)(2,1)S(1)}, bf16[1,128,8192]{2,1,0:T(8,128)(2,1)}, u32[]{:S(2)}) copy-start(bf16[1,128,8192]{2,1,0:T(8,128)(2,1)} %param.4) | copy-start | bytes 6291460
  118.5 1.2 copy-start.6
  118.8 1.0 copy-start.9
  118.8 1.1 copy-start.10
  118.8 1.7 copy-start.8
  120.5 13.7 %all-to-all-start.4 = ((f32[8,32,128]{2,1,0:T(8,128)}), f32[8,32,128]{2,1,0:T(8,128)S(1)}, u32[]{:S(2)}, u32[]{:S(2)}) async-start(f32[8,32,128]{2,1,0:T(8,128)} %broadcast_in_dim.17), calls=%async_computation.4 | async-start | bytes 262144 | tf_op jit(solution)/shard_map/all_to_all | solution.py:273
  125.4 34.5 %collective-permute-start.10 = (bf16[128,4096]{1,0:T(8,128)(2,1)}, bf16[128,4096]{1,0:T(8,128)(2,1)}, u32[]{:S(2)}, u32[]{:S(2)}) collective-permute-start(bf16[128,4096]{1,0:T(8,128)(2,1)} %collective-permute-done.6.refs_5_), channel_id=1, source_target_pairs={{0,1},{1,2},{2,3},{3,4},{4,5},{5,6},{6,7},{7,0},{8,9},{9,10},{10,1... | collective-permute-start | bytes 3145736 | tf_op jit(solution)/shard_map/ppermute | solution.py:37
  126.8 31.2 %collective-permute-start.11 = (bf16[128,4096]{1,0:T(8,128)(2,1)}, bf16[128,4096]{1,0:T(8,128)(2,1)}, u32[]{:S(2)}, u32[]{:S(2)}) collective-permute-start(bf16[128,4096]{1,0:T(8,128)(2,1)} %collective-permute-done.7.refs_2_), channel_id=1, source_target_pairs={{0,7},{1,0},{2,1},{3,2},{4,3},{5,4},{6,5},{7,6},{8,15},{9,8},{10,9... | collective-permute-start | bytes 3145736 | tf_op jit(solution)/shard_map/ppermute | solution.py:37
  140.2 31.4 %all-to-all-start.5 = ((f32[32,32,256]{2,1,0:T(8,128)}), f32[32,32,256]{2,1,0:T(8,128)}, u32[]{:S(2)}, u32[]{:S(2)}) async-start(f32[32,32,256]{2,1,0:T(8,128)} %broadcast_in_dim.18), calls=%async_computation.5 | async-start | bytes 2097152 | tf_op jit(solution)/shard_map/all_to_all | solution.py:280
  151.4 13.0 %copy-start.4 = (bf16[128,4096]{1,0:T(8,128)(2,1)S(1)}, bf16[128,4096]{1,0:T(8,128)(2,1)}, u32[]{:S(2)}) copy-start(bf16[128,4096]{1,0:T(8,128)(2,1)} %copy-done.3) | copy-start | bytes 3145732
  155.3 27.0 %collective-permute-start.12 = (bf16[128,2048]{1,0:T(8,128)(2,1)}, bf16[128,2048]{1,0:T(8,128)(2,1)}, u32[]{:S(2)}, u32[]{:S(2)}) collective-permute-start(bf16[128,2048]{1,0:T(8,128)(2,1)} %slice.101), channel_id=1, source_target_pairs={{0,1},{1,2},{2,3},{3,4},{4,5},{5,6},{6,7},{7,0},{8,9},{9,10},{10,1... | collective-permute-start | bytes 1572872 | tf_op jit(solution)/shard_map/ppermute | solution.py:37
  156.0 26.3 %collective-permute-start.13 = (bf16[128,2048]{1,0:T(8,128)(2,1)}, bf16[128,2048]{1,0:T(8,128)(2,1)}, u32[]{:S(2)}, u32[]{:S(2)}) collective-permute-start(bf16[128,2048]{1,0:T(8,128)(2,1)} %slice.102), channel_id=1, source_target_pairs={{0,7},{1,0},{2,1},{3,2},{4,3},{5,4},{6,5},{7,6},{8,15},{9,8},{10,9... | collective-permute-start | bytes 1572872 | tf_op jit(solution)/shard_map/ppermute | solution.py:37
  161.7 20.5 %collective-permute-start.14 = (bf16[128,2048]{1,0:T(8,128)(2,1)}, bf16[128,2048]{1,0:T(8,128)(2,1)}, u32[]{:S(2)}, u32[]{:S(2)}) collective-permute-start(bf16[128,2048]{1,0:T(8,128)(2,1)} %slice.103), channel_id=1, source_target_pairs={{0,1},{1,2},{2,3},{3,4},{4,5},{5,6},{6,7},{7,0},{8,9},{9,10},{10,1... | collective-permute-start | bytes 1572872 | tf_op jit(solution)/shard_map/ppermute | solution.py:37
  161.7 20.5 %collective-permute-start.15 = (bf16[128,2048]{1,0:T(8,128)(2,1)}, bf16[128,2048]{1,0:T(8,128)(2,1)}, u32[]{:S(2)}, u32[]{:S(2)}) collective-permute-start(bf16[128,2048]{1,0:T(8,128)(2,1)} %slice.104), channel_id=1, source_target_pairs={{0,7},{1,0},{2,1},{3,2},{4,3},{5,4},{6,5},{7,6},{8,15},{9,8},{10,9... | collective-permute-start | bytes 1572872 | tf_op jit(solution)/shard_map/ppermute | solution.py:37
  174.2 2.2 %copy-start.1 = (bf16[1,8192,256]{2,1,0:T(8,128)(2,1)S(1)}, bf16[1,8192,256]{2,1,0:T(8,128)(2,1)}, u32[]{:S(2)}) copy-start(bf16[1,8192,256]{2,1,0:T(8,128)(2,1)} %param.6) | copy-start | bytes 12582916
  176.4 5.9 %copy-start.2 = (f32[4096,256]{1,0:T(8,128)S(1)}, f32[4096,256]{1,0:T(8,128)}, u32[]{:S(2)}) copy-start(f32[4096,256]{1,0:T(8,128)} %shard_map.60.refs_4_) | copy-start | bytes 12582916
